TPU v7x, 32 devices: a whole 2x2x4 slice. The times are simulated.
32 devices in a mesh: dp: 32 (over z, y, x, core).
Axes of the slice: x: 2, y: 2, z: 4, core: 2. Of those that a mesh axis runs over, the one named last changes fastest.
Arguments:
- tokens: bfloat16 [2560, 37, 384], P('dp'), may hold values from -6 to 6
- layer_gains: float32 [2, 2, 384], replicated, may hold values from 0.5 to 1.5
- layer_shifts: float32 [2, 2, 384], replicated, may hold values from -1.25 to 1.25
- w_qkv: bfloat16 [2, 384, 1152], replicated, may hold values from -0.3125 to 0.3125
- b_qv: float32 [2, 768], replicated, may hold values from -1.25 to 1.25
- w_out: bfloat16 [2, 384, 384], replicated, may hold values from -1.25 to 1.25
- b_out: float32 [2, 384], replicated, may hold values from -1.25 to 1.25
- w_fc1: bfloat16 [2, 384, 1536], replicated, may hold values from -0.3125 to 0.3125
- b_fc1: float32 [2, 1536], replicated, may hold values from -1.25 to 1.25
- w_fc2: bfloat16 [2, 1536, 384], replicated, may hold values from -0.15625 to 0.15625
- b_fc2: float32 [2, 384], replicated, may hold values from -1.25 to 1.25
- final_gain: float32 [384], replicated, may hold values from 0.5 to 1.5
- final_shift: float32 [384], replicated, may hold values from -1.25 to 1.25
- head_w1: bfloat16 [384, 2048], replicated, may hold values from -0.3125 to 0.3125
- head_b1: float32 [2048], replicated, may hold values from -1.25 to 1.25
- head_w2: bfloat16 [2048, 2048], replicated, may hold values from -0.125 to 0.125
- head_b2: float32 [2048], replicated, may hold values from -1.25 to 1.25
- head_w3: bfloat16 [2048, 256], replicated, may hold values from -0.125 to 0.125
- head_b3: float32 [256], replicated, may hold values from -1.25 to 1.25
- prototypes: bfloat16 [256, 8192], P(None, 'dp'), may hold values from -6 to 6
- crop_counts: int32 [256], replicated, may hold values from 2 to 10, as said below
- teacher_logits: float32 [256, 8192], P(None, 'dp'), may hold values from -0.625 to 0.625
- first_epoch: int32 [8192], P('dp'), may hold values 0 or 1
Outputs:
- tokens_grad: float32 [2560, 37, 384], P('dp')
- layer_gains_grad: float32 [2, 2, 384], replicated
- layer_shifts_grad: float32 [2, 2, 384], replicated
- w_qkv_grad: float32 [2, 384, 1152], replicated
- b_qv_grad: float32 [2, 768], replicated
- w_out_grad: float32 [2, 384, 384], replicated
- b_out_grad: float32 [2, 384], replicated
- w_fc1_grad: float32 [2, 384, 1536], replicated
- b_fc1_grad: float32 [2, 1536], replicated
- w_fc2_grad: float32 [2, 1536, 384], replicated
- b_fc2_grad: float32 [2, 384], replicated
- final_gain_grad: float32 [384], replicated
- final_shift_grad: float32 [384], replicated
- head_w1_grad: float32 [384, 2048], P(None, 'dp')
- head_b1_grad: float32 [2048], P('dp')
- head_w2_grad: float32 [2048, 2048], P('dp')
- head_b2_grad: float32 [2048], P('dp')
- head_w3_grad: float32 [2048, 256], P('dp')
- head_b3_grad: float32 [256], replicated
- prototypes_grad: float32 [256, 8192], P(None, 'dp')
Inputs may be any that keep to these rules, and one draw needn't show every extreme that they name: `crop_counts`: every image has from 2 up to 10 local crops, and some image has exactly 10.
All inputs are finite; a program needn't handle non-finite values. No bound on the sum of `first_epoch` on one device may be relied on, other than what follows from the above.
Results may differ from a plain program's by a relative error of at most 0.022.
Values may be sent and summed in bfloat16 or wider, within the bound.
No kernel may reach another device: no remote copies, remote signals or barrier semaphores. Data moves between devices by JAX's collectives and lax.ppermute only.
A program may use at most 384 MiB of HBM per device.

v0:
```python
import jax
import jax.numpy as jnp
from jax import lax
from jax.sharding import PartitionSpec as P

HEADS = 6
HD = 64
MOST_CROPS = 10


STUDENT_TEMP = 0.1
TEACHER_TEMP = 0.04
EPS = 1e-06


def product(left, right):
    return jnp.dot(left, right, preferred_element_type=jnp.float32)


def against(left, right):
    return lax.dot_general(
        left, right, (((1,), (1,)), ((), ())), preferred_element_type=jnp.float32
    )


def inner_rows(left, right):
    return lax.dot_general(
        left, right, (((0,), (0,)), ((), ())), preferred_element_type=jnp.float32
    )


def column_sum(values):
    return jnp.sum(values.astype(jnp.float32), axis=0)


def smooth(values):
    return jax.nn.gelu(values, approximate=False)


def smooth_back(values, grad):
    return jax.vjp(smooth, values)[1](grad)[0]


def norm_forward(values, gain, shift):
    centered = values - jnp.mean(values, axis=-1, keepdims=True)
    rstd = lax.rsqrt(jnp.mean(centered * centered, axis=-1, keepdims=True) + EPS)
    normed = centered * rstd
    return (normed * gain + shift, normed, rstd)


def norm_backward(grad, normed, rstd, gain):
    scaled = grad * gain
    inner = (
        scaled
        - jnp.mean(scaled, axis=-1, keepdims=True)
        - normed * jnp.mean(scaled * normed, axis=-1, keepdims=True)
    )
    return (rstd * inner, jnp.sum(grad * normed, axis=0), jnp.sum(grad, axis=0))


def attend(queries, key_rows, value_rows, scaling):
    scores = (
        jnp.einsum("sqhe,skhe->shqk", queries, key_rows, preferred_element_type=jnp.float32)
        * scaling
    )
    row_top = jnp.max(scores, axis=-1, keepdims=True)
    expo = jnp.exp(scores - row_top)
    row_total = jnp.sum(expo, axis=-1, keepdims=True)
    weights = (expo / row_total).astype(jnp.bfloat16)
    result = jnp.einsum("shqk,skhe->sqhe", weights, value_rows, preferred_element_type=jnp.float32)
    return (result, row_top + jnp.log(row_total))


def attend_back(queries, key_rows, value_rows, logsum, grad_out, scaling):
    scores = (
        jnp.einsum("sqhe,skhe->shqk", queries, key_rows, preferred_element_type=jnp.float32)
        * scaling
    )
    weights = jnp.exp(scores - logsum)
    grad_values = jnp.einsum(
        "shqk,sqhe->skhe",
        weights.astype(jnp.bfloat16),
        grad_out,
        preferred_element_type=jnp.float32,
    )
    grad_weights = jnp.einsum(
        "sqhe,skhe->shqk", grad_out, value_rows, preferred_element_type=jnp.float32
    )
    grad_scores = (
        weights * (grad_weights - jnp.sum(grad_weights * weights, axis=-1, keepdims=True))
    ).astype(jnp.bfloat16)
    grad_queries = (
        jnp.einsum("shqk,skhe->sqhe", grad_scores, key_rows, preferred_element_type=jnp.float32)
        * scaling
    )
    grad_keys = (
        jnp.einsum("shqk,sqhe->skhe", grad_scores, queries, preferred_element_type=jnp.float32)
        * scaling
    )
    return (grad_queries, grad_keys, grad_values)


def with_first(full, first):
    shaped = full.reshape(first.shape[0], -1, full.shape[1])
    leading = shaped[:, :1] + first[:, None]
    return jnp.concatenate([leading, shaped[:, 1:]], axis=1).reshape(full.shape)


def mlp_back(grad_out, act_low, pre_act, norm_low, w_first, w_second):
    grad_low = grad_out.astype(jnp.bfloat16)
    grad_bias2 = column_sum(grad_low)
    grad_weight2 = inner_rows(act_low, grad_low)
    grad_pre = smooth_back(pre_act, against(grad_low, w_second)).astype(jnp.bfloat16)
    grad_bias1 = column_sum(grad_pre)
    grad_weight1 = inner_rows(norm_low, grad_pre)
    return (against(grad_pre, w_first), grad_weight1, grad_bias1, grad_weight2, grad_bias2)


def per_device(
    tokens,
    layer_gains,
    layer_shifts,
    w_qkv,
    b_qv,
    w_out,
    b_out,
    w_fc1,
    b_fc1,
    w_fc2,
    b_fc2,
    final_gain,
    final_shift,
    head_w1,
    head_b1,
    head_w2,
    head_b2,
    head_w3,
    head_b3,
    prototypes,
    crop_counts,
    teacher_logits,
    first_epoch,
):
    slot_count, seq_len, width = tokens.shape
    row_count = slot_count * seq_len
    scaling = HD ** (-0.5)
    devices = lax.axis_size("dp")
    inputs = tokens.reshape(row_count, width).astype(jnp.float32)
    zero_bias = jnp.zeros((width,), jnp.float32)
    ln_a, normed_a, rstd_a = norm_forward(inputs, layer_gains[0, 0], layer_shifts[0, 0])
    ln_a_low = ln_a.astype(jnp.bfloat16)
    bias_a = jnp.concatenate([b_qv[0, :width], zero_bias, b_qv[0, width:]])
    qkv_a = (
        (product(ln_a_low, w_qkv[0]) + bias_a)
        .astype(jnp.bfloat16)
        .reshape(slot_count, seq_len, 3, HEADS, HD)
    )
    query_a, key_a, value_a = (qkv_a[:, :, 0], qkv_a[:, :, 1], qkv_a[:, :, 2])
    attn_a, logsum_a = attend(query_a, key_a, value_a, scaling)
    attn_a_low = attn_a.astype(jnp.bfloat16).reshape(row_count, width)
    middle_a = inputs + product(attn_a_low, w_out[0]) + b_out[0]
    ln_b, normed_b, rstd_b = norm_forward(middle_a, layer_gains[0, 1], layer_shifts[0, 1])
    ln_b_low = ln_b.astype(jnp.bfloat16)
    pre_a = product(ln_b_low, w_fc1[0]) + b_fc1[0]
    act_a_low = smooth(pre_a).astype(jnp.bfloat16)
    lower_out = middle_a + product(act_a_low, w_fc2[0]) + b_fc2[0]
    ln_c, normed_c, rstd_c = norm_forward(lower_out, layer_gains[1, 0], layer_shifts[1, 0])
    ln_c_low = ln_c.astype(jnp.bfloat16)
    kv_bias = jnp.concatenate([zero_bias, b_qv[1, width:]])
    kv_c = (
        (product(ln_c_low, w_qkv[1, :, width:]) + kv_bias)
        .astype(jnp.bfloat16)
        .reshape(slot_count, seq_len, 2, HEADS, HD)
    )
    key_c, value_c = (kv_c[:, :, 0], kv_c[:, :, 1])
    first_low = ln_c_low.reshape(slot_count, seq_len, width)[:, 0]
    query_c = (
        (product(first_low, w_qkv[1, :, :width]) + b_qv[1, :width])
        .astype(jnp.bfloat16)
        .reshape(slot_count, 1, HEADS, HD)
    )
    attn_c, logsum_c = attend(query_c, key_c, value_c, scaling)
    attn_c_low = attn_c.astype(jnp.bfloat16).reshape(slot_count, width)
    first_in = lower_out.reshape(slot_count, seq_len, width)[:, 0]
    middle_c = first_in + product(attn_c_low, w_out[1]) + b_out[1]
    ln_d, normed_d, rstd_d = norm_forward(middle_c, layer_gains[1, 1], layer_shifts[1, 1])
    ln_d_low = ln_d.astype(jnp.bfloat16)
    pre_c = product(ln_d_low, w_fc1[1]) + b_fc1[1]
    act_c_low = smooth(pre_c).astype(jnp.bfloat16)
    class_out = middle_c + product(act_c_low, w_fc2[1]) + b_fc2[1]
    ln_f, normed_f, rstd_f = norm_forward(class_out, final_gain, final_shift)
    ln_f_low = ln_f.astype(jnp.bfloat16)
    hidden_one = product(ln_f_low, head_w1) + head_b1
    smooth_one = smooth(hidden_one).astype(jnp.bfloat16)
    hidden_two = product(smooth_one, head_w2) + head_b2
    smooth_two = smooth(hidden_two).astype(jnp.bfloat16)
    embedding = product(smooth_two, head_w3) + head_b3
    inv_length = lax.rsqrt(jnp.sum(embedding * embedding, axis=1, keepdims=True) + EPS)
    features = (embedding * inv_length).astype(jnp.bfloat16)
    proto_wide = prototypes.astype(jnp.float32)
    col_inv = lax.rsqrt(jnp.sum(proto_wide * proto_wide, axis=0) + EPS)
    unit_low = (proto_wide * col_inv).astype(jnp.bfloat16)
    all_features = lax.all_gather(features, "dp", axis=0, tiled=True)
    logits = product(all_features, unit_low) / STUDENT_TEMP
    row_top = jnp.max(logits, axis=1)
    row_total = jnp.sum(jnp.exp(logits - row_top[:, None]), axis=1)
    teach = teacher_logits / TEACHER_TEMP
    teach_top = jnp.max(teach, axis=1)
    teach_total = jnp.sum(jnp.exp(teach - teach_top[:, None]), axis=1)
    global_top, global_teach = (
        lax.pmax(row_top.astype(jnp.bfloat16), "dp").astype(row_top.dtype),
        lax.pmax(teach_top.astype(jnp.bfloat16), "dp").astype(teach_top.dtype),
    )
    row_total, teach_total = lax.psum(
        (
            row_total * jnp.exp(row_top - global_top),
            teach_total * jnp.exp(teach_top - global_teach),
        ),
        "dp",
    )
    row_top, teach_top = (global_top, global_teach)
    student_probs = jnp.exp(logits - row_top[:, None]) / row_total[:, None]
    target = jnp.exp(teach - teach_top[:, None]) / teach_total[:, None]
    images = target.shape[0]
    local_cols = target.shape[1]
    target_rows = jnp.broadcast_to(target[:, None], (images, MOST_CROPS, local_cols)).reshape(
        images * MOST_CROPS, local_cols
    )
    live = (
        (jnp.arange(MOST_CROPS, dtype=jnp.int32)[None, :] < crop_counts[:, None])
        .astype(jnp.float32)
        .reshape(-1)
    )
    grad_raw = (
        live[:, None] * (student_probs - target_rows) * (1.0 / (STUDENT_TEMP * devices))
    ).astype(jnp.bfloat16)
    grad_unit = inner_rows(all_features, grad_raw)
    grad_proto = col_inv * grad_unit - proto_wide * col_inv**3 * jnp.sum(
        proto_wide * grad_unit, axis=0
    )
    prototypes_grad = grad_proto * (1 - first_epoch).astype(jnp.float32)[None, :]
    grad_feat = lax.psum_scatter(against(grad_raw, unit_low), "dp", scatter_dimension=0, tiled=True)
    grad_embed = inv_length * grad_feat - embedding * inv_length**3 * jnp.sum(
        embedding * grad_feat, axis=1, keepdims=True
    )
    grad_embed_low = grad_embed.astype(jnp.bfloat16)
    grad_hb3 = column_sum(grad_embed_low)
    grad_hw3 = inner_rows(smooth_two, grad_embed_low)
    grad_hid2 = smooth_back(hidden_two, against(grad_embed_low, head_w3)).astype(jnp.bfloat16)
    grad_hb2 = column_sum(grad_hid2)
    grad_hw2 = inner_rows(smooth_one, grad_hid2)
    grad_hid1 = smooth_back(hidden_one, against(grad_hid2, head_w2)).astype(jnp.bfloat16)
    grad_hb1 = column_sum(grad_hid1)
    grad_hw1_turned = inner_rows(grad_hid1, ln_f_low)
    grad_class, grad_fgain, grad_fshift = norm_backward(
        against(grad_hid1, head_w1), normed_f, rstd_f, final_gain
    )
    share_w1, head_b1_grad, head_w2_grad, head_b2_grad, head_w3_grad = (
        lax.psum_scatter(grad_hw1_turned, "dp", scatter_dimension=0, tiled=True),
        lax.psum_scatter(grad_hb1, "dp", scatter_dimension=0, tiled=True),
        lax.psum_scatter(grad_hw2, "dp", scatter_dimension=0, tiled=True),
        lax.psum_scatter(grad_hb2, "dp", scatter_dimension=0, tiled=True),
        lax.psum_scatter(grad_hw3, "dp", scatter_dimension=0, tiled=True),
    )
    head_w1_grad = share_w1.T
    grad_norm_d, grad_wfc1_c, grad_bfc1_c, grad_wfc2_c, grad_bfc2_c = mlp_back(
        grad_class, act_c_low, pre_c, ln_d_low, w_fc1[1], w_fc2[1]
    )
    grad_mid_in, grad_gain_d, grad_shift_d = norm_backward(
        grad_norm_d, normed_d, rstd_d, layer_gains[1, 1]
    )
    grad_middle_c = grad_class + grad_mid_in
    grad_attn_low = grad_middle_c.astype(jnp.bfloat16)
    grad_bout_c = column_sum(grad_attn_low)
    grad_wout_c = inner_rows(attn_c_low, grad_attn_low)
    grad_attended = (
        against(grad_attn_low, w_out[1]).astype(jnp.bfloat16).reshape(slot_count, 1, HEADS, HD)
    )
    grad_q_c, grad_k_c, grad_v_c = attend_back(
        query_c, key_c, value_c, logsum_c, grad_attended, scaling
    )
    grad_q_low = grad_q_c.reshape(slot_count, width).astype(jnp.bfloat16)
    grad_kv_low = jnp.concatenate(
        [grad_k_c.reshape(row_count, width), grad_v_c.reshape(row_count, width)], axis=1
    ).astype(jnp.bfloat16)
    grad_qkv_c = jnp.concatenate(
        [inner_rows(first_low, grad_q_low), inner_rows(ln_c_low, grad_kv_low)], axis=1
    )
    grad_bqv_c = jnp.concatenate([column_sum(grad_q_low), column_sum(grad_kv_low[:, width:])])
    grad_norm_c = with_first(
        against(grad_kv_low, w_qkv[1, :, width:]), against(grad_q_low, w_qkv[1, :, :width])
    )
    grad_low_in, grad_gain_c, grad_shift_c = norm_backward(
        grad_norm_c, normed_c, rstd_c, layer_gains[1, 0]
    )
    grad_lower_out = with_first(grad_low_in, grad_middle_c)
    upper_parts = (
        jnp.stack([grad_gain_c, grad_gain_d]),
        jnp.stack([grad_shift_c, grad_shift_d]),
        grad_qkv_c,
        grad_bqv_c,
        grad_wout_c,
        grad_bout_c,
        grad_wfc1_c,
        grad_bfc1_c,
        grad_wfc2_c,
        grad_bfc2_c,
    )
    grad_norm_b, grad_wfc1_a, grad_bfc1_a, grad_wfc2_a, grad_bfc2_a = mlp_back(
        grad_lower_out, act_a_low, pre_a, ln_b_low, w_fc1[0], w_fc2[0]
    )
    grad_mid_a_in, grad_gain_b, grad_shift_b = norm_backward(
        grad_norm_b, normed_b, rstd_b, layer_gains[0, 1]
    )
    grad_middle_a = grad_lower_out + grad_mid_a_in
    grad_attn_a_low = grad_middle_a.astype(jnp.bfloat16)
    grad_bout_a = column_sum(grad_attn_a_low)
    grad_wout_a = inner_rows(attn_a_low, grad_attn_a_low)
    grad_attended_a = (
        against(grad_attn_a_low, w_out[0])
        .astype(jnp.bfloat16)
        .reshape(slot_count, seq_len, HEADS, HD)
    )
    grad_q_a, grad_k_a, grad_v_a = attend_back(
        query_a, key_a, value_a, logsum_a, grad_attended_a, scaling
    )
    grad_qkv_low = jnp.concatenate(
        [
            grad_q_a.reshape(row_count, width),
            grad_k_a.reshape(row_count, width),
            grad_v_a.reshape(row_count, width),
        ],
        axis=1,
    ).astype(jnp.bfloat16)
    grad_qkv_a = inner_rows(ln_a_low, grad_qkv_low)
    grad_bqv_a = jnp.concatenate(
        [column_sum(grad_qkv_low[:, :width]), column_sum(grad_qkv_low[:, 2 * width :])]
    )
    grad_input_in, grad_gain_a, grad_shift_a = norm_backward(
        against(grad_qkv_low, w_qkv[0]), normed_a, rstd_a, layer_gains[0, 0]
    )
    tokens_grad = (grad_middle_a + grad_input_in).reshape(slot_count, seq_len, width)
    lower_parts = (
        jnp.stack([grad_gain_a, grad_gain_b]),
        jnp.stack([grad_shift_a, grad_shift_b]),
        grad_qkv_a,
        grad_bqv_a,
        grad_wout_a,
        grad_bout_a,
        grad_wfc1_a,
        grad_bfc1_a,
        grad_wfc2_a,
        grad_bfc2_a,
    )
    joined = tuple(
        (
            jnp.stack([lower_item, upper_item])
            for lower_item, upper_item in zip(lower_parts, upper_parts)
        )
    )
    summed = lax.psum(
        (
            joined[0],
            joined[1],
            joined[2],
            joined[3],
            joined[4],
            joined[5],
            joined[6],
            joined[7],
            joined[8],
            joined[9],
            grad_fgain,
            grad_fshift,
            grad_hb3,
        ),
        "dp",
    )
    stacked = summed[:10]
    final_gain_grad, final_shift_grad, head_b3_grad = (summed[10], summed[11], summed[12])
    return (
        tokens_grad,
        stacked[0],
        stacked[1],
        stacked[2],
        stacked[3],
        stacked[4],
        stacked[5],
        stacked[6],
        stacked[7],
        stacked[8],
        stacked[9],
        final_gain_grad,
        final_shift_grad,
        head_w1_grad,
        head_b1_grad,
        head_w2_grad,
        head_b2_grad,
        head_w3_grad,
        head_b3_grad,
        prototypes_grad,
    )


def solution(mesh):
    return jax.shard_map(
        per_device,
        mesh=mesh,
        in_specs=(
            P("dp", None, None),
            P(),
            P(),
            P(),
            P(),
            P(),
            P(),
            P(),
            P(),
            P(),
            P(),
            P(),
            P(),
            P(),
            P(),
            P(),
            P(),
            P(),
            P(),
            P(None, "dp"),
            P(),
            P(None, "dp"),
            P("dp"),
        ),
        out_specs=(
            P("dp", None, None),
            P(),
            P(),
            P(),
            P(),
            P(),
            P(),
            P(),
            P(),
            P(),
            P(),
            P(),
            P(),
            P(None, "dp"),
            P("dp"),
            P("dp", None),
            P("dp"),
            P("dp", None),
            P(),
            P(None, "dp"),
        ),
        check_vma=False,
    )
```

profile of v0, /device:TPU:0, one launch (start us, length us, event | category | flops | bytes accessed | tf_op | source)
XLA Modules:
  0.0 1492.1 jit_solution(12846866243988117390)
XLA Ops:
  24.6 8.5 fusion.7
  33.1 21.0 %reshape.429 = bf16[80,37,3,6,64]{4,3,2,1,0:T(8,128)(2,1)} reshape(bf16[2960,1152]{1,0:T(8,128)(2,1)} %fusion.7) | data formatting | bytes 13639680 | tf_op jit(solution)/shard_map/reshape | solution.py:156
  54.1 14.5 fusion.173
  68.6 11.3 multiply_reduce_fusion.1
  79.9 6.7 fusion.8
  86.6 11.1 convert_bitcast_fusion.1
  97.7 6.2 copy.98
  103.9 8.3 reshape.430
  112.2 5.8 reshape.448
  126.9 46.1 %multiply_convert_fusion = (bf16[2960,1536]{1,0:T(8,128)(2,1)S(1)}, f32[2960,1536]{1,0:T(8,128)}, f32[2960,1536]{1,0:T(8,128)}) fusion(f32[1536]{0:T(1024)S(1)} %get-tuple-element.99, bf16[2,384,1536]{2,1,0:T(8,128)(2,1)S(1)} %copy-done.141, f32[2960,384]{1,0:T(8,128)S(1)} %get-tuple-element.178, f32[384]{0:T(512)S(1)} %get-tuple-element.105, ...), kind=kOutput, calls=%fused_computation.5 | convolution fusion | flops 3797514240 | bytes 51228672 | tf_op jit(solution)/shard_map/dot_general | solution.py:17
  173.1 7.2 fusion.175
  180.3 5.4 reshape.434
  196.4 6.4 add_convert_fusion.1
  202.8 14.8 reshape.433
  217.6 11.0 slice_bitcast_fusion
  231.8 5.5 fusion.37
  258.1 55.4 %all-gather.2.cloned.1.call-done = bf16[2560,256]{1,0:T(8,128)(2,1)} async-done(((bf16[80,256]{1,0:T(8,128)(2,1)}), bf16[2560,256]{1,0:T(8,128)(2,1)}) %all-gather.2.cloned.1.call-update) | async-done | bytes 1310736 | tf_op jit(solution)/shard_map/all_gather | solution.py:203
  317.3 39.3 %all-reduce.6 = (bf16[256]{0:T(256)(128)(2,1)S(1)}, bf16[2560]{0:T(1024)(128)(2,1)S(1)}) all-reduce(bf16[256]{0:T(256)(128)(2,1)S(1)} %convert_element_type.247, bf16[2560]{0:T(1024)(128)(2,1)S(1)} %convert_element_type.245), channel_id=1, replica_groups=mesh['dp'=32] {'dp'}, use_global_device_ids=true, to_apply=%region_21.0 | all-reduce | flops 2816 | bytes 11264 | tf_op jit(solution)/shard_map/pmax | solution.py:212
  356.6 40.4 %all-reduce.4 = (f32[256]{0:T(256)S(1)}, f32[2560]{0:T(1024)S(1)}) all-reduce(f32[256]{0:T(256)S(1)} %exponential_multiply_fusion.1, f32[2560]{0:T(1024)S(1)} %exponential_multiply_fusion), channel_id=1, replica_groups=mesh['dp'=32] {'dp'}, use_global_device_ids=true, to_apply=%region_23.0 | all-reduce | flops 2816 | bytes 22528 | tf_op jit(solution)/shard_map/psum | solution.py:214
  420.8 130.2 %reduce-scatter.5.cloned.1.call-done = f32[80,256]{1,0:T(8,128)} async-done(((f32[2560,256]{1,0:T(8,128)}), f32[80,256]{1,0:T(8,128)}) %reduce-scatter.5.cloned.1.call-update) | async-done | bytes 81936 | tf_op jit(solution)/shard_map/reduce_scatter | solution.py:242
  556.4 7.2 convert_reduce_fusion.8
  577.4 5.3 fusion.31
  582.8 12.9 fusion.179
  605.7 6.7 copy.104
  612.4 5.5 copy.108
  618.0 5.2 fusion.10
  623.2 8.1 copy.107
  631.3 5.4 copy.109
  636.7 5.0 fusion.19
  649.2 5.4 reshape.438
  654.6 5.4 multiply_reduce_fusion.2
  660.3 7.4 subtract_multiply_fusion.1
  667.7 5.6 reshape.439
  682.2 5.4 reshape.440
  691.7 22.4 %convert_reduce_fusion = (f32[1536]{0:T(1024)S(1)}, bf16[2960,1536]{1,0:T(8,128)(2,1)}) fusion(f32[2960,1536]{1,0:T(8,128)} %get-tuple-element.159, bf16[2960,384]{1,0:T(8,128)(2,1)} %convert_element_type.262, bf16[2,1536,384]{2,1,0:T(8,128)(2,1)} %param.32, f32[2960,1536]{1,0:T(8,128)} %get-tuple-element.179, f32[1536]{0:T(1024)S(1)} %copy-done.104), kind=kOutput, calls=%fused_computation.3 | convolution fusion | flops 3569048064 | bytes 48930816 | tf_op jit(solution)/shard_map/dot_general | solution.py:21
  714.1 12.0 multiply_reduce_fusion.3
  726.1 5.4 convert_reduce_fusion.2
  736.8 7.9 reshape.441
  744.8 10.4 convert_bitcast_fusion
  755.2 15.4 %multiply_reduce_fusion = (f32[80,6,37]{2,1,0:T(8,128)S(1)}, f32[80,6,37,37]{2,3,1,0:T(8,128)}) fusion(f32[80,6,37,37]{2,3,1,0:T(8,128)} %get-tuple-element.176, f32[80,6,37]{2,1,0:T(8,128)S(1)} %log_add_fusion, bf16[80,37,1,6,64]{4,3,2,1,0:T(8,128)(2,1)} %get-tuple-element.160, bf16[80,37,6,64]{3,2,1,0:T(8,128)(2,1)} %reshape.441), kind=kOutput, calls=%fused_computation.25 | convolution fusion | flops 86722080 | bytes 9945600 | tf_op jit(solution)/shard_map/sqhe,skhe->shqk/dot_general | solution.py:86
  770.5 10.3 multiply_convert_fusion.4
  780.9 9.1 fusion.15
  789.9 9.1 fusion.14
  799.4 6.2 copy.122
  805.6 8.5 reshape.447
  814.1 8.3 reshape.446
  822.4 6.2 copy.120
  828.7 8.3 reshape.444
  837.0 6.1 copy.118
  843.1 8.4 reshape.443
  851.5 6.2 copy.117
  857.7 8.5 reshape.442
  877.2 5.2 fusion.23
  883.8 7.7 convolution_bitcast_fusion.3
  894.6 9.2 convolution_bitcast_fusion.4
  916.7 8.1 fusion.181
  934.5 10.3 multiply_reduce_fusion.4
  945.1 39.0 %all-reduce.3 = (f32[2,2,384]{2,1,0:T(2,128)}, f32[2,2,384]{2,1,0:T(2,128)}, f32[2,768]{1,0:T(2,128)}, f32[2,384]{1,0:T(2,128)}, f32[2,1536]{1,0:T(2,128)}, /*in...) all-reduce(f32[2,2,384]{2,1,0:T(2,128)S(1)} %pad_maximum_fusion.8, ...), channel_id=1, replica_groups=mesh['dp'=32] {'dp'}, use_global_device_ids=true, to_apply=%region_42.0 | all-reduce | flops 14336 | bytes 114688 | tf_op jit(solution)/shard_map/psum | solution.py:361
  985.3 8.5 multiply_add_fusion
  993.8 5.4 reshape.445
  999.2 5.4 copy.124
  1004.6 30.7 %reduce-scatter.11.cloned.1.call-done = f32[64,256]{1,0:T(8,128)} async-done(((f32[2048,256]{1,0:T(8,128)}), f32[64,256]{1,0:T(8,128)}) %reduce-scatter.11.cloned.1.call-update) | async-done | bytes 65552 | tf_op jit(solution)/shard_map/reduce_scatter | solution.py:263
  1035.3 253.2 %all-reduce.9.cloned.1.call-done = (f32[2,384,1152]{2,1,0:T(8,128)}, f32[2,384,384]{2,1,0:T(8,128)}, f32[2,384,1536]{2,1,0:T(8,128)}, f32[2,1536,384]{2,1,0:T(8,128)}) async-done(((f32[2,384,1152]{2,1,0:T(8,128)}, f32[2,384,384]{2,1,0:T(8,128)}, f32[2,384,1536]{2,1,0:T(8,128)}, f32[2,1536,384]{2,1,0:T(8,128)}), (f32[2,384,1152]{2,1,0:T(8,128)}, f32[2,384,384]{2,1,0:T(8,128)}, f32[2,384,1536]{2,1,0:T(8,128)}, ...) | async-done | bytes 14155792 | tf_op jit(solution)/shard_map/psum | solution.py:361
  1288.5 185.6 %reduce-scatter.9.cloned.1.call-done = f32[64,2048]{1,0:T(8,128)} async-done(((f32[2048,2048]{1,0:T(8,128)}), f32[64,2048]{1,0:T(8,128)}) %reduce-scatter.9.cloned.1.call-update) | async-done | bytes 524304 | tf_op jit(solution)/shard_map/reduce_scatter | solution.py:261
  (504 shorter events, 192.9 us)
Async XLA Ops:
  7.2 239.3 %copy-start = (bf16[384,2048]{1,0:T(8,128)(2,1)S(1)}, bf16[384,2048]{1,0:T(8,128)(2,1)}, u32[]{:S(2)}) copy-start(bf16[384,2048]{1,0:T(8,128)(2,1)} %param.36) | copy-start | bytes 4718596
  7.2 306.4 %all-gather.2.cloned.1.call-start = ((), (), s32[]{:S(2)}) async-start(), calls=%async_computation.4 | async-start | bytes 1351680 | tf_op jit(solution)/shard_map/all_gather | solution.py:203
  16.3 109.6 %copy-start.91 = (f32[384]{0:T(512)}, f32[384]{0:T(512)S(1)}, u32[]{:S(2)}) copy-start(f32[384]{0:T(512)S(1)} %get-tuple-element.211) | copy-start | bytes 4612
  16.3 109.6 %copy-start.127 = (f32[384]{0:T(512)}, f32[384]{0:T(512)S(1)}, u32[]{:S(2)}) copy-start(f32[384]{0:T(512)S(1)} %get-tuple-element.105) | copy-start | bytes 4612
  86.6 11.1 copy-start.35
  123.5 49.5 %copy-start.4 = (f32[2960,384]{1,0:T(8,128)}, f32[2960,384]{1,0:T(8,128)S(1)}, u32[]{:S(2)}) copy-start(f32[2960,384]{1,0:T(8,128)S(1)} %get-tuple-element.178) | copy-start | bytes 13639684
  123.6 49.4 %copy-start.69 = (f32[2960]{0:T(1024)}, f32[2960]{0:T(1024)S(1)}, u32[]{:S(2)}) copy-start(f32[2960]{0:T(1024)S(1)} %broadcast_multiply_fusion.8) | copy-start | bytes 35524
  124.7 48.4 %copy-start.72 = (f32[2960]{0:T(1024)}, f32[2960]{0:T(1024)S(1)}, u32[]{:S(2)}) copy-start(f32[2960]{0:T(1024)S(1)} %add_rsqrt_fusion.2) | copy-start | bytes 35524
  125.3 47.8 %copy-start.103 = (f32[1536]{0:T(1024)}, f32[1536]{0:T(1024)S(1)}, u32[]{:S(2)}) copy-start(f32[1536]{0:T(1024)S(1)} %get-tuple-element.99) | copy-start | bytes 18436
  126.9 46.2 %copy-start.139 = (bf16[2,1536,384]{2,1,0:T(8,128)(2,1)S(1)}, bf16[2,1536,384]{2,1,0:T(8,128)(2,1)}, u32[]{:S(2)}) copy-start(bf16[2,1536,384]{2,1,0:T(8,128)(2,1)} %param.32) | copy-start | bytes 7077892
  173.1 7.2 copy-start.145
  217.6 12.7 copy-start.129
  250.0 7.1 copy-start.137
  250.0 7.3 copy-start.19
  255.6 57.9 %copy-start.126 = (f32[80]{0:T(128)}, f32[80]{0:T(128)S(1)}, u32[]{:S(2)}) copy-start(f32[80]{0:T(128)S(1)} %get-tuple-element.174) | copy-start | bytes 964
  256.5 294.5 %reduce-scatter.5.cloned.1.call-start = ((), (), s32[]{:S(2)}) async-start(), calls=%async_computation.5 | async-start | bytes 2703360 | tf_op jit(solution)/shard_map/reduce_scatter | solution.py:242
  258.1 152.3 %copy-start.86 = (f32[256]{0:T(256)}, f32[256]{0:T(256)S(1)}, u32[]{:S(2)}) copy-start(f32[256]{0:T(256)S(1)} %get-tuple-element.172) | copy-start | bytes 3076
  413.6 591.0 %reduce-scatter.7.cloned.1.call-start = ((), (), s32[]{:S(2)}) async-start(), calls=%async_computation.6 | async-start | bytes 3244032 | tf_op jit(solution)/shard_map/reduce_scatter | solution.py:259
  556.4 7.3 copy-start.40
  556.4 8.0 copy-start.31
  556.4 8.0 copy-start.80
  556.4 8.0 copy-start.111
  556.4 8.0 copy-start.119
  556.4 8.0 copy-start.125
  566.7 10.1 copy-start.26
  570.7 12.0 copy-start.43
  573.5 9.3 copy-start.57
  573.5 9.3 copy-start.29
  573.5 9.3 copy-start.66
  600.9 42.1 %copy-start.48 = (bf16[80,6,64]{0,2,1:T(8,128)(2,1)}, bf16[80,6,64]{0,2,1:T(8,128)(2,1)S(1)}, u32[]{:S(2)}) copy-start(bf16[80,6,64]{0,2,1:T(8,128)(2,1)S(1)} %get-tuple-element.151) | copy-start | bytes 184324
  691.7 22.4 %copy-start.70 = (f32[2960]{0:T(1024)S(1)}, f32[2960]{0:T(1024)}, u32[]{:S(2)}) copy-start(f32[2960]{0:T(1024)} %copy-done.69) | copy-start | bytes 35524
  691.7 22.4 %copy-start.73 = (f32[2960]{0:T(1024)S(1)}, f32[2960]{0:T(1024)}, u32[]{:S(2)}) copy-start(f32[2960]{0:T(1024)} %copy-done.72) | copy-start | bytes 35524
  691.7 22.4 %copy-start.92 = (f32[384]{0:T(512)S(1)}, f32[384]{0:T(512)}, u32[]{:S(2)}) copy-start(f32[384]{0:T(512)} %copy-done.91) | copy-start | bytes 4612
  714.1 12.0 copy-start.12
  726.1 7.5 copy-start.27
  789.9 9.2 copy-start.47
  799.1 236.2 %reduce-scatter.11.cloned.1.call-start = ((), (), s32[]{:S(2)}) async-start(), calls=%async_computation.8 | async-start | bytes 2162688 | tf_op jit(solution)/shard_map/reduce_scatter | solution.py:263
  857.7 8.6 copy-start.44
  857.7 8.6 copy-start.60
  857.7 10.5 copy-start.34
  857.7 10.5 copy-start.58
  857.7 10.5 copy-start.84
  857.7 10.5 copy-start.94
  857.7 10.5 copy-start.117
  857.7 10.5 copy-start.135
  874.0 9.7 slice-start.2
  883.8 7.7 copy-start.14
  894.0 394.5 %all-reduce.9.cloned.1.call-start = ((), (), s32[]{:S(2)}) async-start(), calls=%async_computation.9 | async-start | bytes 28311552 | tf_op jit(solution)/shard_map/psum | solution.py:361
  894.6 9.2 copy-start.13
  915.7 558.4 %reduce-scatter.9.cloned.1.call-start = ((), (), s32[]{:S(2)}) async-start(), calls=%async_computation.7 | async-start | bytes 17301504 | tf_op jit(solution)/shard_map/reduce_scatter | solution.py:261
  924.9 7.2 copy-start.85
  927.1 7.2 copy-start.77
  934.4 10.4 copy-start.133
  934.4 10.4 copy-start.96
  934.4 10.4 copy-start.97
  934.4 10.4 copy-start.132
  934.4 10.4 copy-start.112
  934.4 10.5 copy-start.131
  934.4 10.6 copy-start.78
  934.4 10.6 copy-start.102
  934.4 10.6 copy-start.108
  934.5 10.6 copy-start.109
  934.5 10.6 copy-start.120
  1288.5 189.8 %copy-start.42 = (f32[2,384,384]{2,1,0:T(8,128)S(1)}, f32[2,384,384]{2,1,0:T(8,128)}, u32[]{:S(2)}) copy-start(f32[2,384,384]{2,1,0:T(8,128)} %get-tuple-element.218) | copy-start | bytes 3538948
  (98 other events, 339.4 us)
Sparse Core Ops, SparseCore 0:
  256.6 56.9 all-gather.1
  413.7 137.2 reduce-scatter.4
  799.2 97.4 reduce-scatter.6
  899.4 135.8 reduce-scatter.10
  1043.8 244.6 all-reduce.8
  1291.3 182.7 reduce-scatter.8
where the time goes:
time: 1500 us; the launch traced here: 1490 us
  waiting for transfers between devices  655 us (44%)
  local copies, waits for them, and re-layouts  292 us (19%)
  matrix products  291 us (19%)
  blocking collectives  119 us (8%)
  other arithmetic  117 us (8%)
  between operations  16.3 us (1%)
    psum x1, waiting for transfers between devices, per_device(): lax.psum((joined[0], joined[1], joined[2], joined[3], joined[4], joined[5...  253 us
    reduce_scatter x1, waiting for transfers between devices, per_device(): lax.psum_scatter(grad_hw2, 'dp', scatter_dimension=0, tiled=True)  186 us
    reduce_scatter x1, waiting for transfers between devices, per_device(): lax.psum_scatter(against(grad_raw, unit_low), 'dp', scatter_dimension=0,...  130 us
    dot_general x13, matrix products, product(): return jnp.dot(left, right, preferred_element_type=jnp.float32)  87.6 us
    dot_general x13, matrix products, against(): lax.dot_general(left, right, (((1,), (1,)), ((), ())), preferred_element_...  73.9 us
    all_gather x1, waiting for transfers between devices, per_device(): all_features = lax.all_gather(features, 'dp', axis=0, tiled=True)  55.4 us
    dot_general x13, matrix products, inner_rows(): lax.dot_general(left, right, (((0,), (0,)), ((), ())), preferred_element_...  46.6 us
    psum x1, blocking collectives, per_device(): lax.psum((row_total * jnp.exp(row_top - global_top), teach_total * jnp.ex...  40.4 us
  transfers between devices with their start and end apart: 6, of which 5 were waited for; matrix products, arithmetic and copies ran while one was open for 11% of the time, Pallas kernels for 0%

commit v1 on v0

v1 whole, which is shorter than its diff:
```python
import jax
import jax.numpy as jnp
from jax import lax
from jax.experimental import pallas as pl
from jax.experimental.pallas import tpu as pltpu
from jax.sharding import PartitionSpec as P

HEADS = 6
HD = 64
MOST_CROPS = 10


STUDENT_TEMP = 0.1
TEACHER_TEMP = 0.04
EPS = 1e-06
SHIFT = 10.0


def product(left, right):
    return jnp.dot(left, right, preferred_element_type=jnp.float32)


def against(left, right):
    return lax.dot_general(
        left, right, (((1,), (1,)), ((), ())), preferred_element_type=jnp.float32
    )


def inner_rows(left, right):
    return lax.dot_general(
        left, right, (((0,), (0,)), ((), ())), preferred_element_type=jnp.float32
    )


def column_sum(values):
    return jnp.sum(values.astype(jnp.float32), axis=0)


def smooth(values):
    return jax.nn.gelu(values, approximate=False)


def smooth_back(values, grad):
    return jax.vjp(smooth, values)[1](grad)[0]


def norm_forward(values, gain, shift):
    centered = values - jnp.mean(values, axis=-1, keepdims=True)
    rstd = lax.rsqrt(jnp.mean(centered * centered, axis=-1, keepdims=True) + EPS)
    normed = centered * rstd
    return (normed * gain + shift, normed, rstd)


def norm_backward(grad, normed, rstd, gain):
    scaled = grad * gain
    inner = (
        scaled
        - jnp.mean(scaled, axis=-1, keepdims=True)
        - normed * jnp.mean(scaled * normed, axis=-1, keepdims=True)
    )
    return (rstd * inner, jnp.sum(grad * normed, axis=0), jnp.sum(grad, axis=0))


def mlp_back(grad_out, act_low, pre_act, norm_low, w_first, w_second):
    grad_low = grad_out.astype(jnp.bfloat16)
    grad_bias2 = column_sum(grad_low)
    grad_weight2 = inner_rows(act_low, grad_low)
    grad_pre = smooth_back(pre_act, against(grad_low, w_second)).astype(jnp.bfloat16)
    grad_bias1 = column_sum(grad_pre)
    grad_weight1 = inner_rows(norm_low, grad_pre)
    return (against(grad_pre, w_first), grad_weight1, grad_bias1, grad_weight2, grad_bias2)


def axis_bits(n):
    bits = n.bit_length() - 1
    assert n == 1 << bits
    return bits


def swap(values, bit, n):
    return lax.ppermute(values, "dp", [(i, i ^ (1 << bit)) for i in range(n)])


def gather_any(block, n):
    out = block[None]
    for bit in reversed(range(axis_bits(n))):
        out = jnp.concatenate([out, swap(out, bit, n)], axis=0)
    return out


def gather_ordered(block, n):
    me = lax.axis_index("dp")
    bits = axis_bits(n)
    out = block
    for bit in reversed(range(bits)):
        other = swap(out, bit, n)
        first = ((me >> bit) & 1) == 0
        out = jnp.stack([jnp.where(first, out, other), jnp.where(first, other, out)])
    order = tuple(reversed(range(bits))) + tuple(range(bits, bits + block.ndim))
    return out.transpose(order).reshape((n,) + block.shape)


def scatter_sum(parts, n, wire):
    me = lax.axis_index("dp")
    bits = axis_bits(n)
    out = parts.reshape((2,) * bits + parts.shape[1:])
    for bit in range(bits):
        axis = bits - 1 - bit
        mine = (me >> bit) & 1
        keep = lax.dynamic_index_in_dim(out, mine, axis, keepdims=False)
        send = lax.dynamic_index_in_dim(out, 1 - mine, axis, keepdims=False).astype(wire)
        out = keep + swap(send, bit, n).astype(keep.dtype)
    return out


def sum_all(values, n):
    me = lax.axis_index("dp")
    bits = axis_bits(n)
    out = values
    for bit in range(bits):
        half = out.shape[0] // 2
        mine = (me >> bit) & 1
        keep = lax.dynamic_slice_in_dim(out, mine * half, half, 0)
        send = lax.dynamic_slice_in_dim(out, (1 - mine) * half, half, 0)
        out = keep + swap(send, bit, n)
    for bit in reversed(range(bits)):
        other = swap(out, bit, n)
        first = ((me >> bit) & 1) == 0
        out = jnp.concatenate([jnp.where(first, out, other), jnp.where(first, other, out)], axis=0)
    return out


def sum_small(values, n):
    out = values
    for bit in range(axis_bits(n)):
        out = out + swap(out, bit, n)
    return out


GROUP = 8
PITCH = 40
PAIR = 2 * PITCH
NEVER = -1e30


def smooth_both(values):
    size = jnp.abs(values)
    bell = jnp.exp(values * values * -0.5)
    t = 1.0 / (1.0 + 0.23164189 * size)
    tail = t * (0.127414796 + t * (-0.142248368 + t * (0.7107068705 + t * (-0.7265760135 + t * 0.5307027145))))
    upper = tail * bell
    area = jnp.where(values >= 0, 1.0 - upper, upper)
    return values * area, area + values * (bell * 0.3989422804014327)


def standardize(values):
    centered = values - jnp.mean(values, axis=-1, keepdims=True)
    rstd = lax.rsqrt(jnp.mean(centered * centered, axis=-1, keepdims=True) + EPS)
    return centered * rstd, rstd


def standard_back(grad, normed, rstd, gain):
    scaled = grad * gain
    return rstd * (
        scaled
        - jnp.mean(scaled, axis=-1, keepdims=True)
        - normed * jnp.mean(scaled * normed, axis=-1, keepdims=True)
    )


def fold_rows(values):
    return jnp.sum(values.reshape(-1, 8, values.shape[1]), axis=0)


def both_heads(values):
    lane = lax.broadcasted_iota(jnp.int32, values.shape, 1)
    zero = jnp.zeros_like(values)
    return jnp.concatenate([jnp.where(lane < HD, values, zero), jnp.where(lane < HD, zero, values)])


def join_heads(values):
    rows = values.shape[0] // 2
    lane = lax.broadcasted_iota(jnp.int32, (rows, values.shape[1]), 1)
    return jnp.where(lane < HD, values[:rows], values[rows:])


def spread_heads(values):
    lane = lax.broadcasted_iota(jnp.int32, values.shape, 1) // HD
    return jnp.concatenate([jnp.where(lane == h, values, 0.0) for h in range(HEADS)])


def gather_heads(values):
    lane = lax.broadcasted_iota(jnp.int32, (GROUP, values.shape[1]), 1) // HD
    out = jnp.zeros((GROUP, values.shape[1]), values.dtype)
    for h in range(HEADS):
        out = jnp.where(lane == h, values[h * GROUP : (h + 1) * GROUP], out)
    return out


def soft_columns(scores):
    expo = jnp.exp(scores - jnp.max(scores, axis=0, keepdims=True))
    return expo * (1.0 / jnp.sum(expo, axis=0, keepdims=True))


def take_slots(all_ref, rows_ref, step, seq_len, slots):
    for s in range(GROUP):
        for c in range(all_ref.shape[0]):
            rows_ref[s * PITCH : s * PITCH + seq_len, c * 128 : (c + 1) * 128] = all_ref[
                c, pl.ds(step * GROUP + s, seq_len, stride=slots), :
            ]


def first_rows(ref):
    return jnp.concatenate([ref[s * PITCH : s * PITCH + 1, :] for s in range(GROUP)])


def add_first_rows(ref, values):
    for s in range(GROUP):
        ref[s * PITCH : s * PITCH + 1, :] += values[s : s + 1]


def widen_tokens(tok_ref, all_ref):
    seq_len, slots, width = tok_ref.shape

    @pl.loop(0, seq_len)
    def _(t):
        wide = tok_ref[t].astype(jnp.float32)
        for c in range(all_ref.shape[0]):
            all_ref[c, pl.ds(pl.multiple_of(t * slots, 8), slots), :] = wide[:, c * 128 : (c + 1) * 128]


def forward_kernel(
    tok_ref, pair_mask_ref, class_mask_ref, gains_ref, shifts_ref,
    w_qkv_ref, b_qkv_ref, w_out_ref, b_out_ref, w_fc1_ref, b_fc1_ref, w_fc2_ref, b_fc2_ref,
    w_up_ref, b_up_ref,
    qkv_ref, o_ref, mid_ref, act_ref, slope_ref, x1_ref, kv_ref, cq_ref, co_ref, ch_ref, cx_ref,
    all_ref, x_ref, low_ref, wide_ref,
):
    step = pl.program_id(0)
    seq_len, slots, width = tok_ref.shape
    rows = GROUP * PITCH
    hidden = w_fc1_ref.shape[1]

    @pl.when(step == 0)
    def _():
        widen_tokens(tok_ref, all_ref)
        x_ref[...] = jnp.zeros_like(x_ref)

    take_slots(all_ref, x_ref, step, seq_len, slots)
    chunk = PAIR
    for r in range(0, rows, chunk):
        normed, _ = standardize(x_ref[r : r + chunk, :])
        low_ref[r : r + chunk, :] = (normed * gains_ref[0:1, :] + shifts_ref[0:1, :]).astype(jnp.bfloat16)
    for j in range(3):
        cols = slice(j * width, (j + 1) * width)
        part = product(low_ref[...], w_qkv_ref[:, cols]) + b_qkv_ref[:, cols]
        if j == 0:
            part = part.astype(jnp.bfloat16) * jnp.bfloat16(HD ** -0.5)
        qkv_ref[:, cols] = part.astype(jnp.bfloat16)
    for r in range(0, rows, PAIR):
        for c in range(0, width, 2 * HD):
            keys = qkv_ref[r : r + PAIR, width + c : width + c + 2 * HD]
            values = qkv_ref[r : r + PAIR, 2 * width + c : 2 * width + c + 2 * HD]
            queries = both_heads(qkv_ref[r : r + PAIR, c : c + 2 * HD])
            probs = soft_columns(against(keys, queries) + pair_mask_ref[...]).astype(jnp.bfloat16)
            o_ref[r : r + PAIR, c : c + 2 * HD] = join_heads(inner_rows(probs, values)).astype(jnp.bfloat16)
    mixed = product(o_ref[...], w_out_ref[...])
    for r in range(0, rows, chunk):
        part = x_ref[r : r + chunk, :] + mixed[r : r + chunk] + b_out_ref[...]
        mid_ref[r : r + chunk, :] = part
        normed, _ = standardize(part)
        low_ref[r : r + chunk, :] = (normed * gains_ref[1:2, :] + shifts_ref[1:2, :]).astype(jnp.bfloat16)
    for c in range(0, hidden, 256):
        pre = product(low_ref[...], w_fc1_ref[:, c : c + 256])
        for r in range(0, rows, 32):
            act, slope = smooth_both(pre[r : r + 32] + b_fc1_ref[:, c : c + 256])
            act_ref[r : r + 32, c : c + 256] = act.astype(jnp.bfloat16)
            slope_ref[r : r + 32, c : c + 256] = slope.astype(jnp.bfloat16)
    mixed = product(act_ref[...], w_fc2_ref[...])
    for r in range(0, rows, chunk):
        part = mid_ref[r : r + chunk, :] + mixed[r : r + chunk] + b_fc2_ref[...]
        x1_ref[r : r + chunk, :] = part
        normed, _ = standardize(part)
        wide = normed * gains_ref[2:3, :] + shifts_ref[2:3, :]
        wide_ref[r : r + chunk, :] = wide
        low_ref[r : r + chunk, :] = wide.astype(jnp.bfloat16)
    for j in range(2):
        cols = slice(j * width, (j + 1) * width)
        ups = slice((j + 1) * width, (j + 2) * width)
        kv_ref[:, cols] = (product(low_ref[...], w_up_ref[:, ups]) + b_up_ref[:, ups]).astype(jnp.bfloat16)
    cx_ref[...] = first_rows(x1_ref)
    first = first_rows(wide_ref).astype(jnp.bfloat16)
    ch_ref[...] = first.astype(jnp.float32)
    query = (product(first, w_up_ref[:, :width]) + b_up_ref[:, :width]).astype(jnp.bfloat16).astype(jnp.float32) * HD ** -0.5
    cq_ref[...] = query
    spread = spread_heads(query).astype(jnp.bfloat16)
    probs = soft_columns(against(kv_ref[:, :width], spread) + class_mask_ref[...]).astype(jnp.bfloat16)
    co_ref[...] = gather_heads(inner_rows(probs, kv_ref[:, width:]))


def upper_back_kernel(
    class_mask_ref, gains_ref, shifts_ref, w_up_ref, x1_ref, kv_ref, cq_ref, cg_ref, cres_ref,
    dx_ref, dq_ref, dw_ref, vec_ref,
    acc_ref, wide_ref,
):
    step = pl.program_id(0)
    rows, width = x1_ref.shape

    @pl.when(step == 0)
    def _():
        acc_ref[...] = jnp.zeros_like(acc_ref)
        vec_ref[...] = jnp.zeros_like(vec_ref)

    keys, values = kv_ref[:, :width], kv_ref[:, width:]
    spread = spread_heads(cq_ref[...]).astype(jnp.bfloat16)
    grads = spread_heads(cg_ref[...]).astype(jnp.bfloat16)
    probs = soft_columns(against(keys, spread) + class_mask_ref[...])
    back = against(values, grads)
    inner = (probs * (back - jnp.sum(back * probs, axis=0, keepdims=True))).astype(jnp.bfloat16)
    grad_values = product(probs.astype(jnp.bfloat16), grads).astype(jnp.bfloat16)
    grad_keys = product(inner, spread).astype(jnp.bfloat16)
    grad_query = (gather_heads(inner_rows(inner, keys)) * HD ** -0.5).astype(jnp.bfloat16)
    dq_ref[...] = grad_query.astype(jnp.float32)
    vec_ref[:, :width] += fold_rows(grad_values.astype(jnp.float32))
    wide_ref[...] = against(grad_keys, w_up_ref[:, width : 2 * width]) + against(grad_values, w_up_ref[:, 2 * width :])
    add_first_rows(wide_ref, against(grad_query, w_up_ref[:, :width]))
    chunk = PAIR
    parts = []
    for r in range(0, rows, chunk):
        normed, rstd = standardize(x1_ref[r : r + chunk, :])
        parts.append((normed * gains_ref[2:3, :] + shifts_ref[2:3, :]).astype(jnp.bfloat16))
        grad = wide_ref[r : r + chunk, :]
        vec_ref[:, width : 2 * width] += fold_rows(grad * normed)
        vec_ref[:, 2 * width : 3 * width] += fold_rows(grad)
        dx_ref[r : r + chunk, :] = standard_back(grad, normed, rstd, gains_ref[2:3, :])
    turned = jnp.concatenate(parts).T
    acc_ref[:, :width] += product(turned, grad_keys)
    acc_ref[:, width:] += product(turned, grad_values)
    add_first_rows(dx_ref, cres_ref[...])

    @pl.when(step == pl.num_programs(0) - 1)
    def _():
        dw_ref[...] = acc_ref[...].astype(jnp.bfloat16)


def mlp_back_kernel(
    gains_ref, shifts_ref, w_fc1_ref, w_fc2_ref, dx_ref, mid_ref, act_ref, slope_ref,
    dmid_ref, dw1_ref, dw2_ref, vec_ref, vec1_ref,
    acc1_ref, acc2_ref, dz_ref,
):
    step = pl.program_id(0)
    rows, width = dx_ref.shape
    hidden = act_ref.shape[1]

    @pl.when(step == 0)
    def _():
        acc1_ref[...] = jnp.zeros_like(acc1_ref)
        acc2_ref[...] = jnp.zeros_like(acc2_ref)
        vec_ref[...] = jnp.zeros_like(vec_ref)
        vec1_ref[...] = jnp.zeros_like(vec1_ref)

    low = dx_ref[...].astype(jnp.bfloat16)
    vec_ref[:, :width] += fold_rows(low.astype(jnp.float32))
    low_turned = low.T
    chunk = PAIR
    parts = []
    for r in range(0, rows, chunk):
        normed, _ = standardize(mid_ref[r : r + chunk, :])
        parts.append((normed * gains_ref[1:2, :] + shifts_ref[1:2, :]).astype(jnp.bfloat16))
    norm_turned = jnp.concatenate(parts).T
    for c in range(0, hidden, 256):
        cols = slice(c, c + 256)
        back = against(low, w_fc2_ref[cols, :])
        for r in range(0, rows, chunk):
            part = (back[r : r + chunk] * slope_ref[r : r + chunk, cols].astype(jnp.float32)).astype(jnp.bfloat16)
            dz_ref[r : r + chunk, cols] = part
            vec1_ref[:, cols] += fold_rows(part.astype(jnp.float32))
        acc1_ref[:, cols] += product(norm_turned, dz_ref[:, cols])
        acc2_ref[:, cols] += product(low_turned, act_ref[:, cols])
    mixed = against(dz_ref[...], w_fc1_ref[...])
    for r in range(0, rows, chunk):
        normed, rstd = standardize(mid_ref[r : r + chunk, :])
        grad = mixed[r : r + chunk]
        vec_ref[:, width : 2 * width] += fold_rows(grad * normed)
        vec_ref[:, 2 * width : 3 * width] += fold_rows(grad)
        dmid_ref[r : r + chunk, :] = dx_ref[r : r + chunk, :] + standard_back(grad, normed, rstd, gains_ref[1:2, :])

    @pl.when(step == pl.num_programs(0) - 1)
    def _():
        dw1_ref[...] = acc1_ref[...].astype(jnp.bfloat16)
        dw2_ref[...] = acc2_ref[...].T.astype(jnp.bfloat16)


def attend_back_kernel(
    tok_ref, pair_mask_ref, gains_ref, shifts_ref, w_qkv_ref, w_out_ref, dmid_ref, qkv_ref, o_ref,
    dtok_ref, dwo_ref, dwqkv_ref, vec_ref,
    all_ref, out_ref, x_ref, acco_ref, accqkv_ref, do_ref, dqkv_ref,
):
    step = pl.program_id(0)
    seq_len, slots, width = tok_ref.shape
    rows = GROUP * PITCH

    @pl.when(step == 0)
    def _():
        widen_tokens(tok_ref, all_ref)
        x_ref[...] = jnp.zeros_like(x_ref)
        acco_ref[...] = jnp.zeros_like(acco_ref)
        accqkv_ref[...] = jnp.zeros_like(accqkv_ref)
        vec_ref[...] = jnp.zeros_like(vec_ref)

    take_slots(all_ref, x_ref, step, seq_len, slots)
    low = dmid_ref[...].astype(jnp.bfloat16)
    vec_ref[:, :width] += fold_rows(low.astype(jnp.float32))
    do_ref[...] = against(low, w_out_ref[...]).astype(jnp.bfloat16)
    acco_ref[...] += product(o_ref[...].T, low)
    for r in range(0, rows, PAIR):
        for c in range(0, width, 2 * HD):
            keys = qkv_ref[r : r + PAIR, width + c : width + c + 2 * HD]
            values = qkv_ref[r : r + PAIR, 2 * width + c : 2 * width + c + 2 * HD]
            queries = both_heads(qkv_ref[r : r + PAIR, c : c + 2 * HD])
            grads = both_heads(do_ref[r : r + PAIR, c : c + 2 * HD])
            probs = soft_columns(against(keys, queries) + pair_mask_ref[...])
            back = against(values, grads)
            inner = (probs * (back - jnp.sum(back * probs, axis=0, keepdims=True))).astype(jnp.bfloat16)
            dqkv_ref[r : r + PAIR, 2 * width + c : 2 * width + c + 2 * HD] = product(
                probs.astype(jnp.bfloat16), grads
            ).astype(jnp.bfloat16)
            dqkv_ref[r : r + PAIR, width + c : width + c + 2 * HD] = product(inner, queries).astype(jnp.bfloat16)
            dqkv_ref[r : r + PAIR, c : c + 2 * HD] = (
                join_heads(inner_rows(inner, keys)) * HD ** -0.5
            ).astype(jnp.bfloat16)
    chunk = PAIR
    parts = []
    for r in range(0, rows, chunk):
        normed, _ = standardize(x_ref[r : r + chunk, :])
        parts.append((normed * gains_ref[0:1, :] + shifts_ref[0:1, :]).astype(jnp.bfloat16))
    turned = jnp.concatenate(parts).T
    for j in range(3):
        cols = slice(j * width, (j + 1) * width)
        vec_ref[:, (j + 1) * width : (j + 2) * width] += fold_rows(dqkv_ref[:, cols].astype(jnp.float32))
        accqkv_ref[:, cols] += product(turned, dqkv_ref[:, cols])
    mixed = against(dqkv_ref[...], w_qkv_ref[...])
    for r in range(0, rows, chunk):
        normed, rstd = standardize(x_ref[r : r + chunk, :])
        grad = mixed[r : r + chunk]
        vec_ref[:, 4 * width : 5 * width] += fold_rows(grad * normed)
        vec_ref[:, 5 * width : 6 * width] += fold_rows(grad)
        part = dmid_ref[r : r + chunk, :] + standard_back(grad, normed, rstd, gains_ref[0:1, :])
        for s in range(chunk // PITCH):
            for t in range(all_ref.shape[0]):
                out_ref[t, pl.ds(step * GROUP + r // PITCH + s, seq_len, stride=slots), :] = part[
                    s * PITCH : s * PITCH + seq_len, t * 128 : (t + 1) * 128
                ]

    @pl.when(step == pl.num_programs(0) - 1)
    def _():
        for t in range(out_ref.shape[0]):
            dtok_ref[:, t * 128 : (t + 1) * 128] = out_ref[t]
        dwo_ref[...] = acco_ref[...].astype(jnp.bfloat16)
        dwqkv_ref[...] = accqkv_ref[...].astype(jnp.bfloat16)


def whole(array):
    return pl.BlockSpec(array.shape, lambda i: (0,) * len(array.shape))


def by_step(rows, width):
    return pl.BlockSpec((rows, width), lambda i: (i, 0))


def run_kernel(body, steps, whole_in, step_in, outs, scratch, flops):
    in_specs = [whole(a) for a in whole_in] + [by_step(rows, a.shape[1]) for a, rows in step_in]
    out_specs = [
        by_step(rows, shape[1]) if rows else pl.BlockSpec(shape, lambda i, k=len(shape): (0,) * k)
        for shape, dtype, rows in outs
    ]
    return pl.pallas_call(
        body,
        grid=(steps,),
        in_specs=in_specs,
        out_specs=out_specs,
        out_shape=[jax.ShapeDtypeStruct(shape, dtype) for shape, dtype, rows in outs],
        scratch_shapes=scratch,
        compiler_params=pltpu.CompilerParams(
            dimension_semantics=("arbitrary",), vmem_limit_bytes=56 * 1024 * 1024
        ),
        cost_estimate=pl.CostEstimate(flops=flops, bytes_accessed=40 * 1024 * 1024, transcendentals=0),
    )(*whole_in, *[a for a, rows in step_in])


def score_masks(seq_len):
    key = jnp.arange(PAIR)[:, None]
    query = (jnp.arange(2 * PAIR) % PAIR)[None, :]
    pair = (key // PITCH == query // PITCH) & (key % PITCH < seq_len)
    key = jnp.arange(GROUP * PITCH)[:, None]
    column = (jnp.arange(HEADS * GROUP) % GROUP)[None, :]
    single = (key // PITCH == column) & (key % PITCH < seq_len)
    return [jnp.where(m, 0.0, NEVER).astype(jnp.float32) for m in (pair, single)]


def per_device(
    tokens,
    layer_gains,
    layer_shifts,
    w_qkv,
    b_qv,
    w_out,
    b_out,
    w_fc1,
    b_fc1,
    w_fc2,
    b_fc2,
    final_gain,
    final_shift,
    head_w1,
    head_b1,
    head_w2,
    head_b2,
    head_w3,
    head_b3,
    prototypes,
    crop_counts,
    teacher_logits,
    first_epoch,
):
    slot_count, seq_len, width = tokens.shape
    row_count = slot_count * seq_len
    scaling = HD ** (-0.5)
    devices = lax.axis_size("dp")
    proto_wide = prototypes.astype(jnp.float32)
    col_inv = lax.rsqrt(jnp.sum(proto_wide * proto_wide, axis=0) + EPS)
    unit_low = (proto_wide * col_inv).astype(jnp.bfloat16)
    unit_all = gather_any(unit_low.T, devices).reshape(-1, unit_low.shape[0])
    teach_expo = jnp.exp(teacher_logits * (1.0 / TEACHER_TEMP))
    teach_part = jnp.concatenate(
        [
            against(teach_expo.astype(jnp.bfloat16), unit_low),
            jnp.broadcast_to(jnp.sum(teach_expo, axis=1, keepdims=True), (teach_expo.shape[0], 128)),
        ],
        axis=1,
    )
    teach_sum = scatter_sum(
        teach_part.reshape(devices, -1, teach_part.shape[1]), devices, jnp.float32
    )
    live = (
        (jnp.arange(MOST_CROPS, dtype=jnp.int32)[None, :] < crop_counts[:, None])
        .astype(jnp.float32)
        .reshape(-1)
    )
    zero_bias = jnp.zeros((width,), jnp.float32)
    pair_mask, class_mask = score_masks(seq_len)
    gains = jnp.pad(layer_gains.reshape(4, width), ((0, 4), (0, 0)))
    shifts = jnp.pad(layer_shifts.reshape(4, width), ((0, 4), (0, 0)))
    full_bias = [jnp.concatenate([b_qv[l, :width], zero_bias, b_qv[l, width:]])[None] for l in range(2)]
    turned_tokens = tokens.transpose(1, 0, 2)
    steps = slot_count // GROUP
    rows = GROUP * PITCH
    padded = slot_count * PITCH
    hidden = w_fc1.shape[2]
    low, wide = jnp.bfloat16, jnp.float32
    qkv_a, attn_a, middle_a, act_a, slope_a, lower_out, kv_c, query_c, attn_c, first_low, first_in = run_kernel(
        forward_kernel,
        steps,
        [turned_tokens, pair_mask, class_mask, gains, shifts, w_qkv[0], full_bias[0], w_out[0], b_out[:1], w_fc1[0], b_fc1[:1], w_fc2[0], b_fc2[:1], w_qkv[1], full_bias[1]],
        [],
        [
            ((padded, 3 * width), low, rows),
            ((padded, width), low, rows),
            ((padded, width), wide, rows),
            ((padded, hidden), low, rows),
            ((padded, hidden), low, rows),
            ((padded, width), wide, rows),
            ((padded, 2 * width), low, rows),
            ((slot_count, width), wide, GROUP),
            ((slot_count, width), wide, GROUP),
            ((slot_count, width), wide, GROUP),
            ((slot_count, width), wide, GROUP),
        ],
        [
            pltpu.VMEM((width // 128, row_count, 128), wide),
            pltpu.VMEM((rows, width), wide),
            pltpu.VMEM((rows, width), low),
            pltpu.VMEM((rows, width), wide),
        ],
        12 * 10**9,
    )
    first_low = first_low.astype(low)
    attn_c_low = attn_c.astype(low)
    middle_c = first_in + product(attn_c_low, w_out[1]) + b_out[1]
    ln_d, normed_d, rstd_d = norm_forward(middle_c, layer_gains[1, 1], layer_shifts[1, 1])
    ln_d_low = ln_d.astype(jnp.bfloat16)
    pre_c = product(ln_d_low, w_fc1[1]) + b_fc1[1]
    act_c_low = smooth(pre_c).astype(jnp.bfloat16)
    class_out = middle_c + product(act_c_low, w_fc2[1]) + b_fc2[1]
    ln_f, normed_f, rstd_f = norm_forward(class_out, final_gain, final_shift)
    ln_f_low = ln_f.astype(jnp.bfloat16)
    hidden_one = product(ln_f_low, head_w1) + head_b1
    smooth_one = smooth(hidden_one).astype(jnp.bfloat16)
    hidden_two = product(smooth_one, head_w2) + head_b2
    smooth_two = smooth(hidden_two).astype(jnp.bfloat16)
    embedding = product(smooth_two, head_w3) + head_b3
    inv_length = lax.rsqrt(jnp.sum(embedding * embedding, axis=1, keepdims=True) + EPS)
    features = (embedding * inv_length).astype(jnp.bfloat16)
    all_features = gather_ordered(features, devices).reshape(-1, features.shape[1])
    logits = against(features, unit_all) * (1.0 / STUDENT_TEMP)
    expo = jnp.exp(logits - SHIFT)
    row_total = jnp.sum(expo, axis=1)
    own_live = lax.dynamic_slice_in_dim(live, lax.axis_index("dp") * slot_count, slot_count, 0)
    student_feat = product(expo.astype(jnp.bfloat16), unit_all) / row_total[:, None]
    teach_feat = teach_sum[:, : features.shape[1]] / teach_sum[:, features.shape[1] :][:, :1]
    grad_feat = (
        own_live[:, None]
        * (student_feat - jnp.repeat(teach_feat, MOST_CROPS, axis=0))
        * (1.0 / (STUDENT_TEMP * devices))
    )
    totals = gather_ordered(
        jnp.concatenate([row_total, teach_sum[:, features.shape[1]]])[None], devices
    ).reshape(devices, -1)
    all_row_total = totals[:, :slot_count].reshape(-1)
    all_teach_total = totals[:, slot_count:].reshape(-1)
    all_logits = product(all_features, unit_low) * (1.0 / STUDENT_TEMP)
    student_probs = jnp.exp(all_logits - SHIFT) / all_row_total[:, None]
    target = teach_expo / all_teach_total[:, None]
    images, local_cols = target.shape
    target_rows = jnp.broadcast_to(target[:, None], (images, MOST_CROPS, local_cols)).reshape(
        images * MOST_CROPS, local_cols
    )
    grad_raw = (
        live[:, None] * (student_probs - target_rows) * (1.0 / (STUDENT_TEMP * devices))
    ).astype(jnp.bfloat16)
    grad_unit = inner_rows(all_features, grad_raw)
    grad_proto = col_inv * grad_unit - proto_wide * col_inv**3 * jnp.sum(
        proto_wide * grad_unit, axis=0
    )
    prototypes_grad = grad_proto * (1 - first_epoch).astype(jnp.float32)[None, :]
    grad_embed = inv_length * grad_feat - embedding * inv_length**3 * jnp.sum(
        embedding * grad_feat, axis=1, keepdims=True
    )
    grad_embed_low = grad_embed.astype(jnp.bfloat16)
    grad_hb3 = column_sum(grad_embed_low)
    grad_hw3 = inner_rows(smooth_two, grad_embed_low)
    grad_hid2 = smooth_back(hidden_two, against(grad_embed_low, head_w3)).astype(jnp.bfloat16)
    grad_hb2 = column_sum(grad_hid2)
    grad_hw2 = inner_rows(smooth_one, grad_hid2)
    grad_hid1 = smooth_back(hidden_one, against(grad_hid2, head_w2)).astype(jnp.bfloat16)
    grad_hb1 = column_sum(grad_hid1)
    grad_hw1_turned = inner_rows(grad_hid1, ln_f_low)
    grad_class, grad_fgain, grad_fshift = norm_backward(
        against(grad_hid1, head_w1), normed_f, rstd_f, final_gain
    )
    head_parts = jnp.concatenate(
        [
            grad_hw1_turned.astype(jnp.bfloat16),
            grad_hw2.astype(jnp.bfloat16),
            grad_hw3.astype(jnp.bfloat16),
            jnp.broadcast_to(grad_hb1.astype(jnp.bfloat16)[:, None], (grad_hb1.shape[0], 128)),
            jnp.broadcast_to(grad_hb2.astype(jnp.bfloat16)[:, None], (grad_hb2.shape[0], 128)),
        ],
        axis=1,
    )
    head_sum = scatter_sum(
        head_parts.reshape(devices, -1, head_parts.shape[1]), devices, jnp.bfloat16
    ).astype(jnp.float32)
    hid = grad_hw2.shape[1]
    head_w1_grad = head_sum[:, :width].T
    head_w2_grad = head_sum[:, width : width + hid]
    head_w3_grad = head_sum[:, width + hid : width + hid + features.shape[1]]
    head_b1_grad = head_sum[:, width + hid + features.shape[1]]
    head_b2_grad = head_sum[:, width + hid + features.shape[1] + 128]
    grad_norm_d, grad_wfc1_c, grad_bfc1_c, grad_wfc2_c, grad_bfc2_c = mlp_back(
        grad_class, act_c_low, pre_c, ln_d_low, w_fc1[1], w_fc2[1]
    )
    grad_mid_in, grad_gain_d, grad_shift_d = norm_backward(
        grad_norm_d, normed_d, rstd_d, layer_gains[1, 1]
    )
    grad_middle_c = grad_class + grad_mid_in
    grad_attn_low = grad_middle_c.astype(jnp.bfloat16)
    grad_bout_c = column_sum(grad_attn_low)
    grad_wout_c = inner_rows(attn_c_low, grad_attn_low)
    grad_attended = against(grad_attn_low, w_out[1]).astype(low).astype(wide)
    grad_lower_out, grad_q_c, grad_kv_c, vec_c = run_kernel(
        upper_back_kernel,
        steps,
        [class_mask, gains, shifts, w_qkv[1]],
        [(lower_out, rows), (kv_c, rows), (query_c, GROUP), (grad_attended, GROUP), (grad_middle_c, GROUP)],
        [
            ((padded, width), wide, rows),
            ((slot_count, width), wide, GROUP),
            ((width, 2 * width), low, 0),
            ((8, 3 * width), wide, 0),
        ],
        [pltpu.VMEM((width, 2 * width), wide), pltpu.VMEM((rows, width), wide)],
        6 * 10**9,
    )
    grad_q_low = grad_q_c.astype(low)
    vec_c = jnp.sum(vec_c, axis=0)
    upper_parts = (
        jnp.stack([vec_c[width : 2 * width], grad_gain_d]),
        jnp.stack([vec_c[2 * width :], grad_shift_d]),
        jnp.concatenate([inner_rows(first_low, grad_q_low).astype(low), grad_kv_c], axis=1),
        jnp.concatenate([column_sum(grad_q_low), vec_c[:width]]),
        grad_wout_c,
        grad_bout_c,
        grad_wfc1_c,
        grad_bfc1_c,
        grad_wfc2_c,
        grad_bfc2_c,
    )
    grad_middle_a, grad_wfc1_a, grad_wfc2_a, vec_b, vec_hidden = run_kernel(
        mlp_back_kernel,
        steps,
        [gains, shifts, w_fc1[0], w_fc2[0]],
        [(grad_lower_out, rows), (middle_a, rows), (act_a, rows), (slope_a, rows)],
        [
            ((padded, width), wide, rows),
            ((width, hidden), low, 0),
            ((hidden, width), low, 0),
            ((8, 3 * width), wide, 0),
            ((8, hidden), wide, 0),
        ],
        [pltpu.VMEM((width, hidden), wide), pltpu.VMEM((width, hidden), wide), pltpu.VMEM((rows, hidden), low)],
        15 * 10**9,
    )
    grad_tokens, grad_wout_a, grad_qkv_a, vec_a = run_kernel(
        attend_back_kernel,
        steps,
        [turned_tokens, pair_mask, gains, shifts, w_qkv[0], w_out[0]],
        [(grad_middle_a, rows), (qkv_a, rows), (attn_a, rows)],
        [
            ((row_count, width), wide, 0),
            ((width, width), low, 0),
            ((width, 3 * width), low, 0),
            ((8, 6 * width), wide, 0),
        ],
        [
            pltpu.VMEM((width // 128, row_count, 128), wide),
            pltpu.VMEM((width // 128, row_count, 128), wide),
            pltpu.VMEM((rows, width), wide),
            pltpu.VMEM((width, width), wide),
            pltpu.VMEM((width, 3 * width), wide),
            pltpu.VMEM((rows, width), low),
            pltpu.VMEM((rows, 3 * width), low),
        ],
        10 * 10**9,
    )
    tokens_grad = grad_tokens.reshape(seq_len, slot_count, width).transpose(1, 0, 2)
    vec_a, vec_b, vec_hidden = jnp.sum(vec_a, axis=0), jnp.sum(vec_b, axis=0), jnp.sum(vec_hidden, axis=0)
    lower_parts = (
        jnp.stack([vec_a[4 * width : 5 * width], vec_b[width : 2 * width]]),
        jnp.stack([vec_a[5 * width :], vec_b[2 * width :]]),
        grad_qkv_a,
        jnp.concatenate([vec_a[width : 2 * width], vec_a[3 * width : 4 * width]]),
        grad_wout_a,
        vec_a[:width],
        grad_wfc1_a,
        vec_hidden,
        grad_wfc2_a,
        vec_b[:width],
    )

    def bulk(parts):
        return sum_all(
            jnp.concatenate(
                [
                    parts[2].T.astype(jnp.bfloat16),
                    parts[4].astype(jnp.bfloat16),
                    parts[6].T.astype(jnp.bfloat16),
                    parts[8].astype(jnp.bfloat16),
                ]
            ),
            devices,
        ).astype(jnp.float32)

    def small(parts):
        return [parts[0], parts[1], parts[3].reshape(-1, width), parts[5][None], parts[7].reshape(-1, width), parts[9][None]]

    upper_bulk, lower_bulk = bulk(upper_parts), bulk(lower_parts)
    vectors = small(lower_parts) + small(upper_parts) + [grad_fgain[None], grad_fshift[None], jnp.pad(grad_hb3, (0, width - grad_hb3.shape[0]))[None]]
    summed = sum_small(jnp.concatenate(vectors), devices)
    cuts = [0]
    for item in vectors:
        cuts.append(cuts[-1] + item.shape[0])
    pieces = [summed[cuts[i] : cuts[i + 1]] for i in range(len(vectors))]
    both = lambda i: jnp.stack([pieces[i], pieces[i + 6]])
    marks = (0, 3 * width, 4 * width, 4 * width + hidden, 4 * width + 2 * hidden)
    bulk_of = lambda i: [part[marks[i] : marks[i + 1]] for part in (lower_bulk, upper_bulk)]
    return (
        tokens_grad,
        both(0),
        both(1),
        jnp.stack([part.T for part in bulk_of(0)]),
        both(2).reshape(2, -1),
        jnp.stack(bulk_of(1)),
        both(3).reshape(2, -1),
        jnp.stack([part.T for part in bulk_of(2)]),
        both(4).reshape(2, -1),
        jnp.stack(bulk_of(3)),
        both(5).reshape(2, -1),
        summed[cuts[12]],
        summed[cuts[13]],
        head_w1_grad,
        head_b1_grad,
        head_w2_grad,
        head_b2_grad,
        head_w3_grad,
        summed[cuts[14], : grad_hb3.shape[0]],
        prototypes_grad,
    )


def solution(mesh):
    return jax.shard_map(
        per_device,
        mesh=mesh,
        in_specs=(
            P("dp", None, None),
            P(),
            P(),
            P(),
            P(),
            P(),
            P(),
            P(),
            P(),
            P(),
            P(),
            P(),
            P(),
            P(),
            P(),
            P(),
            P(),
            P(),
            P(),
            P(None, "dp"),
            P(),
            P(None, "dp"),
            P("dp"),
        ),
        out_specs=(
            P("dp", None, None),
            P(),
            P(),
            P(),
            P(),
            P(),
            P(),
            P(),
            P(),
            P(),
            P(),
            P(),
            P(),
            P(None, "dp"),
            P("dp"),
            P("dp", None),
            P("dp"),
            P("dp", None),
            P(),
            P(None, "dp"),
        ),
        check_vma=False,
    )
```

time: 1500 us -> 715 us (0.48)
  waiting for transfers between devices: 655 us -> 239 us
  matrix products: 291 us -> 42.2 us
  Pallas kernels: 0 us -> 202 us
  local copies, waits for them, and re-layouts: 292 us -> 107 us
  blocking collectives: 119 us -> 0 us
  other arithmetic: 117 us -> 67.8 us
  starting transfers between devices: 1.29 us -> 46.6 us
    reduce_scatter x4 -> x0, waiting for transfers between devices: 347 us -> none  [the longest x1 186 us: per_device(): lax.psum_scatter(grad_hw2, 'dp', scatter_dimension=0, tiled=True)]
    psum x1 -> x0, waiting for transfers between devices: 253 us -> none  [per_device(): lax.psum((joined[0], joined[1], joined[2], joined[3], joined[4], joined[5...]
    ppermute x0 -> x50, waiting for transfers between devices: none -> 239 us  [swap(): return lax.ppermute(values, 'dp', [(i, i ^ 1 << bit) for i in range(n)])]
    pallas_call x0 -> x4, Pallas kernels: none -> 202 us  [run_kernel(): pl.pallas_call(body, grid=(steps,), in_specs=in_specs, out_specs=out_spec...]
    reshape x15 -> x7, local copies, waits for them, and re-layouts: 125 us -> 0.08 us  [the longest x2 0.02 us: small(): parts[3].reshape(-1, width)]
    dot_general x10 -> x0, matrix products: 83 us -> none  [the longest x2 20.7 us: attend_back(): jnp.einsum('sqhe,skhe->shqk', grad_out, value_rows, preferred_element_typ...]
    psum x2 -> x0, blocking collectives: 79.4 us -> none  [the longest x1 40.4 us: per_device(): lax.psum((row_total * jnp.exp(row_top - global_top), teach_total * jnp.ex...]
    dot_general x13 -> x7, matrix products: 87.6 us -> 11.9 us  [product(): return jnp.dot(left, right, preferred_element_type=jnp.float32)]
  transfers between devices with their start and end apart: 6 -> 50, of which waited for: 5 -> 32; matrix products, arithmetic and copies ran while one was open for 11% -> 23% of each run, Pallas kernels for 0% -> 29%
where the time goes in v1:
time: 715 us; the launch traced here: 708 us
  waiting for transfers between devices  239 us (33%)
  Pallas kernels  202 us (28%)
  local copies, waits for them, and re-layouts  107 us (15%)
  other arithmetic  67.8 us (9%)
  starting transfers between devices  46.6 us (7%)
  matrix products  42.2 us (6%)
    ppermute x50, waiting for transfers between devices, swap(): return lax.ppermute(values, 'dp', [(i, i ^ 1 << bit) for i in range(n)])  239 us
    pallas_call x4, Pallas kernels, run_kernel(): pl.pallas_call(body, grid=(steps,), in_specs=in_specs, out_specs=out_spec...  202 us
    ppermute x50, starting transfers between devices, swap(): return lax.ppermute(values, 'dp', [(i, i ^ 1 << bit) for i in range(n)])  46.6 us
    unnamed x185, local copies, waits for them, and re-layouts  28.6 us
    concatenate x2, local copies, waits for them, and re-layouts, per_device(): jnp.concatenate([grad_hw1_turned.astype(jnp.bfloat16), grad_hw2.astype(jn...  17.3 us
    dot_general x8, matrix products, against(): lax.dot_general(left, right, (((1,), (1,)), ((), ())), preferred_element_...  15.3 us
    dot_general x8, matrix products, inner_rows(): lax.dot_general(left, right, (((0,), (0,)), ((), ())), preferred_element_...  15 us
  transfers between devices with their start and end apart: 50, of which 32 were waited for; matrix products, arithmetic and copies ran while one was open for 23% of the time, Pallas kernels for 29%

profile of v1, /device:TPU:0, one launch (start us, length us, event | category | flops | bytes accessed | tf_op | source)
XLA Modules:
  0.0 707.5 jit_solution(16828440355181191261)
XLA Ops:
  6.7 3.6 collective-permute-start
  15.3 2.5 slice_bitcast_fusion.7.w_fc1_ref
  22.4 82.7 %shard_map.374 = (bf16[3200,1152]{1,0:T(8,128)(2,1)}, bf16[3200,384]{1,0:T(8,128)(2,1)}, f32[3200,384]{1,0:T(8,128)}, bf16[3200,1536]{1,0:T(8,128)(2,1)}, bf16[3...) custom-call(bf16[37,80,384]{2,1,0:T(8,128)(2,1)} %bitcast.298, ...), custom_call_target="tpu_custom_call" | custom-call | flops 12000000000 | bytes 41943040 | tf_op jit(solution)/shard_map/pallas_call | solution.py:477
  106.6 2.2 multiply_convert_fusion.2
  109.5 2.7 multiply_convert_fusion.1
  112.9 3.9 multiply_convert_fusion
  118.7 4.6 collective-permute-done.40
  126.8 2.7 collective-permute-done.41
  129.6 3.7 collective-permute-done.1
  138.7 8.7 %collective-permute-done.2 = bf16[4,256,256]{1,2,0:T(8,128)(2,1)S(1)} collective-permute-done((bf16[4,256,256]{1,2,0:T(8,128)(2,1)S(1)}, bf16[4,256,256]{1,2,0:T(8,128)(2,1)S(1)}, u32[]{:S(2)}, u32[]{:S(2)}) %collective-permute-start.2) | collective-permute-done | bytes 524320 | tf_op jit(solution)/shard_map/ppermute | solution.py:81
  151.0 2.5 collective-permute-done.7
  155.4 12.5 %collective-permute-done.3 = bf16[8,256,256]{1,2,0:T(8,128)(2,1)S(1)} collective-permute-done((bf16[8,256,256]{1,2,0:T(8,128)(2,1)S(1)}, bf16[8,256,256]{1,2,0:T(8,128)(2,1)S(1)}, u32[]{:S(2)}, u32[]{:S(2)}) %collective-permute-start.3) | collective-permute-done | bytes 1048608 | tf_op jit(solution)/shard_map/ppermute | solution.py:81
  173.3 3.4 collective-permute-start.9
  176.7 4.1 collective-permute-done.43
  186.7 3.1 constant_dynamic-update-slice_fusion.5
  189.8 6.9 copy.145
  196.7 3.9 fusion.126
  204.0 6.3 fusion.116
  215.8 1.9 fusion.9
  217.6 3.6 collective-permute-start.45
  221.3 18.4 %shard_map.375 = (f32[3200,384]{1,0:T(8,128)}, f32[80,384]{1,0:T(8,128)}, bf16[384,768]{1,0:T(8,128)(2,1)}, f32[8,1152]{1,0:T(8,128)}) custom-call(f32[320,48]{1,0:T(8,128)} %and_select_fusion.class_mask_ref, f32[8,384]{1,0:T(8,128)} %pad.11.gains_ref, f32[8,384]{1,0:T(8,128)} %pad.12.shifts_ref, bf16[384,1152]{1,0:T(8,128)(2,1)} %get-tuple-element.214.w_up_ref, ...), custom_call_target="tpu_custom_call" | custom-call | flops 6000000000 | bytes 41943040 | tf_op jit(solution)/shard_map/pallas_call | solution.py:477
  240.6 42.6 %shard_map.376 = (f32[3200,384]{1,0:T(8,128)}, bf16[384,1536]{1,0:T(8,128)(2,1)}, bf16[1536,384]{1,0:T(8,128)(2,1)}, f32[8,1152]{1,0:T(8,128)}, f32[8,1536]{1,0:T(8,128)}) custom-call(f32[8,384]{1,0:T(8,128)} %pad.11.gains_ref, f32[8,384]{1,0:T(8,128)} %pad.12.shifts_ref, bf16[384,1536]{1,0:T(8,128)(2,1)} %slice_bitcast_fusion.7.w_fc1_ref, ...), custom_call_target="tpu_custom_call" | custom-call | flops 15000000512 | bytes 41943040 | tf_op jit(solution)/shard_map/pallas_call | solution.py:477
  284.9 58.4 %shard_map.377 = (f32[2960,384]{1,0:T(8,128)}, bf16[384,384]{1,0:T(8,128)(2,1)}, bf16[384,1152]{1,0:T(8,128)(2,1)}, f32[8,2304]{1,0:T(8,128)}) custom-call(bf16[37,80,384]{2,1,0:T(8,128)(2,1)} %bitcast.299, f32[80,160]{1,0:T(8,128)} %and_select_fusion.1.pair_mask_ref, f32[8,384]{1,0:T(8,128)} %pad.11.gains_ref, f32[8,384]{1,0:T(8,128)} %pad.12.shifts_ref, ...), custom_call_target="tpu_custom_call" | custom-call | flops 10000000000 | bytes 41943040 | tf_op jit(solution)/shard_map/pallas_call | solution.py:477
  347.0 2.2 copy.148
  349.3 2.4 copy.147
  353.0 2.0 pad_maximum_fusion.2
  355.0 1.8 copy-done.14
  358.2 11.7 %pad_maximum_fusion.3 = bf16[4608,384]{1,0:T(8,128)(2,1)S(1)} fusion(bf16[1536,384]{1,0:T(8,128)(2,1)S(1)} %convolution_convert_fusion, bf16[1536,384]{1,0:T(8,128)(2,1)S(1)} %convolution_convert_fusion.1, bf16[384,384]{1,0:T(8,128)(2,1)S(1)} %convolution_convert_fusion.4, bf16[1152,384]{1,0:T(8,128)(2,1)S(1)} %maximum_bitcast_fusion.1), kind=kLoop, calls=%fused_computation.18 | loop fusion | flops 14155776 | bytes 7077888 | tf_op jit(solution)/shard_map/concatenate | solution.py:763
  371.9 5.8 convert_dynamic-update-slice_fusion
  383.7 1.9 collective-permute-done.47
  387.4 16.4 %copy.150 = bf16[2048,2944]{1,0:T(8,128)(2,1)} copy(bf16[2048,2944]{0,1:T(8,128)(2,1)} %broadcast_dynamic-update-slice_fusion) | data formatting | bytes 24117248 | tf_op jit(solution)/shard_map/concatenate | solution.py:651
  403.9 5.9 dynamic-slice_bitcast_fusion
  412.6 2.7 collective-permute-done.11
  417.0 2.4 broadcast_in_dim.128
  419.4 5.0 reshape.304
  424.9 3.6 fusion.70
  431.1 3.3 collective-permute-done.14
  435.1 2.6 dynamic-slice_add_fusion.1
  441.2 19.3 %collective-permute-done.16 = bf16[1152,384]{1,0:T(8,128)(2,1)S(1)} collective-permute-done((bf16[1152,384]{1,0:T(8,128)(2,1)S(1)}, bf16[1152,384]{1,0:T(8,128)(2,1)S(1)}, u32[]{:S(2)}, u32[]{:S(2)}) %collective-permute-start.16) | collective-permute-done | bytes 884768 | tf_op jit(solution)/shard_map/ppermute | solution.py:81
  461.4 14.1 %collective-permute-done.26 = bf16[1152,384]{1,0:T(8,128)(2,1)S(1)} collective-permute-done((bf16[1152,384]{1,0:T(8,128)(2,1)S(1)}, bf16[1152,384]{1,0:T(8,128)(2,1)S(1)}, u32[]{:S(2)}, u32[]{:S(2)}) %collective-permute-start.26) | collective-permute-done | bytes 884768 | tf_op jit(solution)/shard_map/ppermute | solution.py:81
  478.8 5.4 collective-permute-done.27
  486.9 4.6 collective-permute-done.28
  491.7 4.4 collective-permute-done.19
  496.4 5.5 collective-permute-done.29
  502.0 2.2 collective-permute-done.20
  504.4 3.7 collective-permute-done.30
  508.2 4.4 collective-permute-done.21
  516.6 8.3 %collective-permute-done.22 = bf16[576,384]{1,0:T(8,128)(2,1)S(1)} collective-permute-done((bf16[576,384]{1,0:T(8,128)(2,1)S(1)}, bf16[576,384]{1,0:T(8,128)(2,1)S(1)}, u32[]{:S(2)}, u32[]{:S(2)}) %collective-permute-start.22) | collective-permute-done | bytes 442400 | tf_op jit(solution)/shard_map/ppermute | solution.py:81
  531.0 15.4 %collective-permute-done.23 = bf16[1152,384]{1,0:T(8,128)(2,1)S(1)} collective-permute-done((bf16[1152,384]{1,0:T(8,128)(2,1)S(1)}, bf16[1152,384]{1,0:T(8,128)(2,1)S(1)}, u32[]{:S(2)}, u32[]{:S(2)}) %collective-permute-start.23) | collective-permute-done | bytes 884768 | tf_op jit(solution)/shard_map/ppermute | solution.py:81
  548.2 7.7 %collective-permute-done.33 = bf16[1152,384]{1,0:T(8,128)(2,1)S(1)} collective-permute-done((bf16[1152,384]{1,0:T(8,128)(2,1)S(1)}, bf16[1152,384]{1,0:T(8,128)(2,1)S(1)}, u32[]{:S(2)}, u32[]{:S(2)}) %collective-permute-start.33) | collective-permute-done | bytes 884768 | tf_op jit(solution)/shard_map/ppermute | solution.py:81
  558.0 5.1 bitcast_add_fusion
  564.8 2.2 broadcast_select_fusion.3
  571.5 2.5 broadcast_select_fusion.1
  575.9 55.1 %collective-permute-done.36 = bf16[2,2,2,64,2944]{4,3,2,1,0:T(8,128)(2,1)S(1)} collective-permute-done((bf16[2,2,2,64,2944]{4,3,2,1,0:T(8,128)(2,1)S(1)}, bf16[2,2,2,64,2944]{4,3,2,1,0:T(8,128)(2,1)S(1)}, u32[]{:S(2)}, u32[]{:S(2)}) %collective-permute-start.36) | collective-permute-done | bytes 3014688 | tf_op jit(solution)/shard_map/ppermute | solution.py:81
  634.4 2.2 pad_maximum_fusion.4
  636.6 5.2 copy.169
  641.7 4.1 slice_bitcast_fusion.1
  645.8 4.2 slice_bitcast_fusion
  650.0 17.2 %collective-permute-done.37 = bf16[2,2,64,2944]{3,2,1,0:T(8,128)(2,1)S(1)} collective-permute-done((bf16[2,2,64,2944]{3,2,1,0:T(8,128)(2,1)S(1)}, bf16[2,2,64,2944]{3,2,1,0:T(8,128)(2,1)S(1)}, u32[]{:S(2)}, u32[]{:S(2)}) %collective-permute-start.37) | collective-permute-done | bytes 1507360 | tf_op jit(solution)/shard_map/ppermute | solution.py:81
  668.4 2.5 pad_maximum_fusion
  670.9 6.2 copy.170
  680.2 5.8 collective-permute-done.38
  687.9 2.5 pad_maximum_fusion.1
  690.4 14.2 %collective-permute-done.39 = bf16[64,2944]{1,0:T(8,128)(2,1)S(1)} collective-permute-done((bf16[64,2944]{1,0:T(8,128)(2,1)S(1)}, bf16[64,2944]{1,0:T(8,128)(2,1)S(1)}, u32[]{:S(2)}, u32[]{:S(2)}) %collective-permute-start.39) | collective-permute-done | bytes 376864 | tf_op jit(solution)/shard_map/ppermute | solution.py:81
  (469 shorter events, 126.8 us)
Async XLA Ops:
  0.7 108.8 %copy-start = (bf16[384,2048]{1,0:T(8,128)(2,1)S(1)}, bf16[384,2048]{1,0:T(8,128)(2,1)}, u32[]{:S(2)}) copy-start(bf16[384,2048]{1,0:T(8,128)(2,1)} %param.36) | copy-start | bytes 4718596
  0.7 12.3 %copy-start.54 = (f32[2,1536]{1,0:T(2,128)S(1)}, f32[2,1536]{1,0:T(2,128)}, u32[]{:S(2)}) copy-start(f32[2,1536]{1,0:T(2,128)} %param.31) | copy-start | bytes 36868
  5.6 130.6 %collective-permute-start.5 = (f32[2,2,2,2,8,384]{5,4,3,2,1,0:T(8,128)}, f32[2,2,2,2,8,384]{5,4,3,2,1,0:T(8,128)}, u32[]{:S(2)}, u32[]{:S(2)}) collective-permute-start(f32[2,2,2,2,8,384]{5,4,3,2,1,0:T(8,128)} %dynamic-slice_bitcast_fusion.5), channel_id=1, source_target_pairs={{0,1},{1,0},{2,3},{3,2},{4,5},{5,4},{6,7},{7,6},{8,9},{9,8},{10,11... | collective-permute-start | bytes 589832 | tf_op jit(solution)/shard_map/ppermute | solution.py:81
  6.7 118.4 %collective-permute-start = (bf16[1,256,256]{1,2,0:T(8,128)(2,1)S(1)}, bf16[1,256,256]{1,2,0:T(8,128)(2,1)S(1)}, u32[]{:S(2)}, u32[]{:S(2)}) collective-permute-start(bf16[1,256,256]{1,2,0:T(8,128)(2,1)S(1)} %get-tuple-element.195), channel_id=1, source_target_pairs={{0,16},{1,17},{2,18},{3,19},{4,20},{5,21},{6,22},{7,23},{8,24},{9,... | collective-permute-start | bytes 393224 | tf_op jit(solution)/shard_map/ppermute | solution.py:81
  22.4 82.7 %copy-start.29 = (bf16[2,384,384]{2,1,0:T(8,128)(2,1)S(1)}, bf16[2,384,384]{2,1,0:T(8,128)(2,1)}, u32[]{:S(2)}) copy-start(bf16[2,384,384]{2,1,0:T(8,128)(2,1)} %param.28) | copy-start | bytes 1769476
  22.4 84.2 %copy-start.43 = (bf16[2,384,1536]{2,1,0:T(8,128)(2,1)S(1)}, bf16[2,384,1536]{2,1,0:T(8,128)(2,1)}, u32[]{:S(2)}) copy-start(bf16[2,384,1536]{2,1,0:T(8,128)(2,1)} %param.30) | copy-start | bytes 7077892
  117.9 5.4 collective-permute-start.40
  124.0 5.5 collective-permute-start.41
  125.2 8.0 %collective-permute-start.1 = (bf16[2,256,256]{1,2,0:T(8,128)(2,1)S(1)}, bf16[2,256,256]{1,2,0:T(8,128)(2,1)S(1)}, u32[]{:S(2)}, u32[]{:S(2)}) collective-permute-start(bf16[2,256,256]{1,2,0:T(8,128)(2,1)S(1)} %pad_maximum_fusion.17), channel_id=1, source_target_pairs={{0,8},{1,9},{2,10},{3,11},{4,12},{5,13},{6,14},{7,15},{8,0},{9,1},... | collective-permute-start | bytes 786440 | tf_op jit(solution)/shard_map/ppermute | solution.py:81
  133.3 14.2 %collective-permute-start.2 = (bf16[4,256,256]{1,2,0:T(8,128)(2,1)S(1)}, bf16[4,256,256]{1,2,0:T(8,128)(2,1)S(1)}, u32[]{:S(2)}, u32[]{:S(2)}) collective-permute-start(bf16[4,256,256]{1,2,0:T(8,128)(2,1)S(1)} %pad_maximum_fusion.12), channel_id=1, source_target_pairs={{0,4},{1,5},{2,6},{3,7},{4,0},{5,1},{6,2},{7,3},{8,12},{9,13},{10,... | collective-permute-start | bytes 1572872 | tf_op jit(solution)/shard_map/ppermute | solution.py:81
  134.9 16.0 %collective-permute-start.42 = (bf16[2,2,80,256]{3,2,1,0:T(8,128)(2,1)S(1)}, bf16[2,2,80,256]{3,2,1,0:T(8,128)(2,1)S(1)}, u32[]{:S(2)}, u32[]{:S(2)}) collective-permute-start(bf16[2,2,80,256]{3,2,1,0:T(8,128)(2,1)S(1)} %pad_maximum_fusion.20), channel_id=1, source_target_pairs={{0,4},{1,5},{2,6},{3,7},{4,0},{5,1},{6,2},{7,3},{8,12},{9,13},{10,... | collective-permute-start | bytes 491528 | tf_op jit(solution)/shard_map/ppermute | solution.py:81
  137.2 12.2 %collective-permute-start.6 = (f32[2,2,2,8,384]{4,3,2,1,0:T(8,128)S(1)}, f32[2,2,2,8,384]{4,3,2,1,0:T(8,128)S(1)}, u32[]{:S(2)}, u32[]{:S(2)}) collective-permute-start(f32[2,2,2,8,384]{4,3,2,1,0:T(8,128)S(1)} %dynamic-slice_bitcast_fusion.6), channel_id=1, source_target_pairs={{0,2},{1,3},{2,0},{3,1},{4,6},{5,7},{6,4},{7,5},{8,10},{9,11},{10,... | collective-permute-start | bytes 294920 | tf_op jit(solution)/shard_map/ppermute | solution.py:81
  147.6 20.3 %collective-permute-start.3 = (bf16[8,256,256]{1,2,0:T(8,128)(2,1)S(1)}, bf16[8,256,256]{1,2,0:T(8,128)(2,1)S(1)}, u32[]{:S(2)}, u32[]{:S(2)}) collective-permute-start(bf16[8,256,256]{1,2,0:T(8,128)(2,1)S(1)} %pad_maximum_fusion.8), channel_id=1, source_target_pairs={{0,2},{1,3},{2,0},{3,1},{4,6},{5,7},{6,4},{7,5},{8,10},{9,11},{10,... | collective-permute-start | bytes 3145736 | tf_op jit(solution)/shard_map/ppermute | solution.py:81
  149.3 4.2 collective-permute-start.7
  169.4 12.3 %copy-start.75 = (s32[256]{0:T(256)S(1)}, s32[256]{0:T(256)}, u32[]{:S(2)}) copy-start(s32[256]{0:T(256)} %param.45) | copy-start | bytes 3076
  169.4 12.9 %copy-start.45 = (f32[256,10]{1,0:T(8,128)S(1)}, f32[256,10]{1,0:T(8,128)}, u32[]{:S(2)}) copy-start(f32[256,10]{1,0:T(8,128)} %fusion.79) | copy-start | bytes 30724
  169.4 17.3 %collective-permute-start.4 = (bf16[16,256,256]{1,2,0:T(8,128)(2,1)}, bf16[16,256,256]{1,2,0:T(8,128)(2,1)}, u32[]{:S(2)}, u32[]{:S(2)}) collective-permute-start(bf16[16,256,256]{1,2,0:T(8,128)(2,1)} %get-tuple-element.218), channel_id=1, source_target_pairs={{0,1},{1,0},{2,3},{3,2},{4,5},{5,4},{6,7},{7,6},{8,9},{9,8},{10,11... | collective-permute-start | bytes 6291464 | tf_op jit(solution)/shard_map/ppermute | solution.py:81
  169.4 3.9 collective-permute-start.8
  170.9 9.8 %collective-permute-start.43 = (bf16[2,2,2,80,256]{4,3,2,1,0:T(8,128)(2,1)S(1)}, bf16[2,2,2,80,256]{4,3,2,1,0:T(8,128)(2,1)S(1)}, u32[]{:S(2)}, u32[]{:S(2)}) collective-permute-start(bf16[2,2,2,80,256]{4,3,2,1,0:T(8,128)(2,1)S(1)} %pad_maximum_fusion.16), channel_id=1, source_target_pairs={{0,2},{1,3},{2,0},{3,1},{4,6},{5,7},{6,4},{7,5},{8,10},{9,11},{10,... | collective-permute-start | bytes 983048 | tf_op jit(solution)/shard_map/ppermute | solution.py:81
  173.3 9.2 %collective-permute-start.9 = (f32[8,384]{1,0:T(8,128)S(1)}, f32[8,384]{1,0:T(8,128)S(1)}, u32[]{:S(2)}, u32[]{:S(2)}) collective-permute-start(f32[8,384]{1,0:T(8,128)S(1)} %dynamic-slice_bitcast_fusion.9), channel_id=1, source_target_pairs={{0,16},{1,17},{2,18},{3,19},{4,20},{5,21},{6,22},{7,23},{8,24},{9,... | collective-permute-start | bytes 36872 | tf_op jit(solution)/shard_map/ppermute | solution.py:81
  181.7 2.4 collective-permute-start.44
  217.6 160.0 %collective-permute-start.45 = (f32[1,88]{1,0:T(1,128)}, f32[1,88]{1,0:T(1,128)}, u32[]{:S(2)}, u32[]{:S(2)}) collective-permute-start(f32[1,88]{1,0:T(1,128)} %maximum_bitcast_fusion.5), channel_id=1, source_target_pairs={{0,16},{1,17},{2,18},{3,19},{4,20},{5,21},{6,22},{7,23},{8,24},{9,... | collective-permute-start | bytes 1064 | tf_op jit(solution)/shard_map/ppermute | solution.py:81
  240.6 44.3 %copy-start.53 = (f32[8,1152]{1,0:T(8,128)S(1)}, f32[8,1152]{1,0:T(8,128)}, u32[]{:S(2)}) copy-start(f32[8,1152]{1,0:T(8,128)} %get-tuple-element.60) | copy-start | bytes 110596
  284.9 59.5 %copy-start.49 = (f32[80,384]{1,0:T(8,128)S(1)}, f32[80,384]{1,0:T(8,128)}, u32[]{:S(2)}) copy-start(f32[80,384]{1,0:T(8,128)} %get-tuple-element.61) | copy-start | bytes 368644
  284.9 59.5 %copy-start.52 = (f32[80,384]{1,0:T(8,128)S(1)}, f32[80,384]{1,0:T(8,128)}, u32[]{:S(2)}) copy-start(f32[80,384]{1,0:T(8,128)} %get-tuple-element.66) | copy-start | bytes 368644
  345.6 64.7 %collective-permute-start.10 = (f32[27,384]{1,0:T(8,128)S(1)}, f32[27,384]{1,0:T(8,128)}, u32[]{:S(2)}, u32[]{:S(2)}) collective-permute-start(f32[27,384]{1,0:T(8,128)S(1)} %concatenate.94), channel_id=1, source_target_pairs={{0,1},{1,0},{2,3},{3,2},{4,5},{5,4},{6,7},{7,6},{8,9},{9,8},{10,11... | collective-permute-start | bytes 124424 | tf_op jit(solution)/shard_map/ppermute | solution.py:81
  371.3 15.2 %copy-start.63 = (bf16[2048]{0:T(1024)(128)(2,1)S(1)}, bf16[2048]{0:T(1024)(128)(2,1)}, u32[]{:S(2)}) copy-start(bf16[2048]{0:T(1024)(128)(2,1)} %get-tuple-element.184) | copy-start | bytes 12292
  371.3 67.1 %collective-permute-start.25 = (bf16[2304,384]{1,0:T(8,128)(2,1)}, bf16[2304,384]{1,0:T(8,128)(2,1)S(1)}, u32[]{:S(2)}, u32[]{:S(2)}) collective-permute-start(bf16[2304,384]{1,0:T(8,128)(2,1)} %constant_dynamic-slice_fusion.4), channel_id=1, source_target_pairs={{0,1},{1,0},{2,3},{3,2},{4,5},{5,4},{6,7},{7,6},{8,9},{9,8},{10,11... | collective-permute-start | bytes 5308424 | tf_op jit(solution)/shard_map/ppermute | solution.py:81
  371.8 63.3 %collective-permute-start.15 = (bf16[2304,384]{1,0:T(8,128)(2,1)}, bf16[2304,384]{1,0:T(8,128)(2,1)}, u32[]{:S(2)}, u32[]{:S(2)}) collective-permute-start(bf16[2304,384]{1,0:T(8,128)(2,1)} %constant_dynamic-slice_fusion.9), channel_id=1, source_target_pairs={{0,1},{1,0},{2,3},{3,2},{4,5},{5,4},{6,7},{7,6},{8,9},{9,8},{10,11... | collective-permute-start | bytes 5308424 | tf_op jit(solution)/shard_map/ppermute | solution.py:81
  378.4 3.6 collective-permute-start.46
  382.0 3.7 collective-permute-start.47
  385.7 18.1 %collective-permute-start.48 = (f32[2,2,2,1,88]{4,2,1,0,3:T(2,128)S(1)}, f32[2,2,2,1,88]{4,2,1,0,3:T(2,128)S(1)}, u32[]{:S(2)}, u32[]{:S(2)}) collective-permute-start(f32[2,2,2,1,88]{4,2,1,0,3:T(2,128)S(1)} %fusion.102), channel_id=1, source_target_pairs={{0,2},{1,3},{2,0},{3,1},{4,6},{5,7},{6,4},{7,5},{8,10},{9,11},{10,... | collective-permute-start | bytes 8456 | tf_op jit(solution)/shard_map/ppermute | solution.py:81
  403.8 6.4 collective-permute-start.49
  403.9 12.9 %copy-start.26 = (f32[256,256]{1,0:T(8,128)S(1)}, f32[256,256]{1,0:T(8,128)}, u32[]{:S(2)}) copy-start(f32[256,256]{1,0:T(8,128)} %param.44) | copy-start | bytes 786436
  409.8 148.2 %collective-permute-start.35 = (bf16[2,2,2,2,64,2944]{5,4,3,2,1,0:T(8,128)(2,1)}, bf16[2,2,2,2,64,2944]{5,4,3,2,1,0:T(8,128)(2,1)}, u32[]{:S(2)}, u32[]{:S(2)}) collective-permute-start(bf16[2,2,2,2,64,2944]{5,4,3,2,1,0:T(8,128)(2,1)} %dynamic-slice_bitcast_fusion), channel_id=1, source_target_pairs={{0,1},{1,0},{2,3},{3,2},{4,5},{5,4},{6,7},{7,6},{8,9},{9,8},{10,11... | collective-permute-start | bytes 18087944 | tf_op jit(solution)/shard_map/ppermute | solution.py:81
  411.1 4.1 collective-permute-start.11
  415.2 9.1 %collective-permute-start.12 = (f32[27,384]{1,0:T(8,128)S(1)}, f32[27,384]{1,0:T(8,128)S(1)}, u32[]{:S(2)}, u32[]{:S(2)}) collective-permute-start(f32[27,384]{1,0:T(8,128)S(1)} %add.419), channel_id=1, source_target_pairs={{0,4},{1,5},{2,6},{3,7},{4,0},{5,1},{6,2},{7,3},{8,12},{9,13},{10,... | collective-permute-start | bytes 124424 | tf_op jit(solution)/shard_map/ppermute | solution.py:81
  424.4 4.3 collective-permute-start.13
  429.5 5.0 collective-permute-start.14
  437.8 22.7 %collective-permute-start.16 = (bf16[1152,384]{1,0:T(8,128)(2,1)S(1)}, bf16[1152,384]{1,0:T(8,128)(2,1)S(1)}, u32[]{:S(2)}, u32[]{:S(2)}) collective-permute-start(bf16[1152,384]{1,0:T(8,128)(2,1)S(1)} %constant_dynamic-slice_fusion.8), channel_id=1, source_target_pairs={{0,2},{1,3},{2,0},{3,1},{4,6},{5,7},{6,4},{7,5},{8,10},{9,11},{10,... | collective-permute-start | bytes 2654216 | tf_op jit(solution)/shard_map/ppermute | solution.py:81
  439.0 36.5 %collective-permute-start.26 = (bf16[1152,384]{1,0:T(8,128)(2,1)S(1)}, bf16[1152,384]{1,0:T(8,128)(2,1)S(1)}, u32[]{:S(2)}, u32[]{:S(2)}) collective-permute-start(bf16[1152,384]{1,0:T(8,128)(2,1)S(1)} %constant_dynamic-slice_fusion.3), channel_id=1, source_target_pairs={{0,2},{1,3},{2,0},{3,1},{4,6},{5,7},{6,4},{7,5},{8,10},{9,11},{10,... | collective-permute-start | bytes 2654216 | tf_op jit(solution)/shard_map/ppermute | solution.py:81
  460.8 16.2 %collective-permute-start.17 = (bf16[576,384]{1,0:T(8,128)(2,1)S(1)}, bf16[576,384]{1,0:T(8,128)(2,1)S(1)}, u32[]{:S(2)}, u32[]{:S(2)}) collective-permute-start(bf16[576,384]{1,0:T(8,128)(2,1)S(1)} %constant_dynamic-slice_fusion.7), channel_id=1, source_target_pairs={{0,4},{1,5},{2,6},{3,7},{4,0},{5,1},{6,2},{7,3},{8,12},{9,13},{10,... | collective-permute-start | bytes 1327112 | tf_op jit(solution)/shard_map/ppermute | solution.py:81
  475.8 8.4 %collective-permute-start.27 = (bf16[576,384]{1,0:T(8,128)(2,1)S(1)}, bf16[576,384]{1,0:T(8,128)(2,1)S(1)}, u32[]{:S(2)}, u32[]{:S(2)}) collective-permute-start(bf16[576,384]{1,0:T(8,128)(2,1)S(1)} %constant_dynamic-slice_fusion.2), channel_id=1, source_target_pairs={{0,4},{1,5},{2,6},{3,7},{4,0},{5,1},{6,2},{7,3},{8,12},{9,13},{10,... | collective-permute-start | bytes 1327112 | tf_op jit(solution)/shard_map/ppermute | solution.py:81
  477.2 8.9 %collective-permute-start.18 = (bf16[288,384]{1,0:T(8,128)(2,1)S(1)}, bf16[288,384]{1,0:T(8,128)(2,1)S(1)}, u32[]{:S(2)}, u32[]{:S(2)}) collective-permute-start(bf16[288,384]{1,0:T(8,128)(2,1)S(1)} %constant_dynamic-slice_fusion.6), channel_id=1, source_target_pairs={{0,8},{1,9},{2,10},{3,11},{4,12},{5,13},{6,14},{7,15},{8,0},{9,1},... | collective-permute-start | bytes 663560 | tf_op jit(solution)/shard_map/ppermute | solution.py:81
  484.3 7.2 %collective-permute-start.28 = (bf16[288,384]{1,0:T(8,128)(2,1)S(1)}, bf16[288,384]{1,0:T(8,128)(2,1)S(1)}, u32[]{:S(2)}, u32[]{:S(2)}) collective-permute-start(bf16[288,384]{1,0:T(8,128)(2,1)S(1)} %constant_dynamic-slice_fusion.1), channel_id=1, source_target_pairs={{0,8},{1,9},{2,10},{3,11},{4,12},{5,13},{6,14},{7,15},{8,0},{9,1},... | collective-permute-start | bytes 663560 | tf_op jit(solution)/shard_map/ppermute | solution.py:81
  486.1 10.0 %collective-permute-start.19 = (bf16[144,384]{1,0:T(8,128)(2,1)S(1)}, bf16[144,384]{1,0:T(8,128)(2,1)S(1)}, u32[]{:S(2)}, u32[]{:S(2)}) collective-permute-start(bf16[144,384]{1,0:T(8,128)(2,1)S(1)} %constant_dynamic-slice_fusion.5), channel_id=1, source_target_pairs={{0,16},{1,17},{2,18},{3,19},{4,20},{5,21},{6,22},{7,23},{8,24},{9,... | collective-permute-start | bytes 331784 | tf_op jit(solution)/shard_map/ppermute | solution.py:81
  491.6 10.2 %collective-permute-start.29 = (bf16[144,384]{1,0:T(8,128)(2,1)S(1)}, bf16[144,384]{1,0:T(8,128)(2,1)S(1)}, u32[]{:S(2)}, u32[]{:S(2)}) collective-permute-start(bf16[144,384]{1,0:T(8,128)(2,1)S(1)} %constant_dynamic-slice_fusion), channel_id=1, source_target_pairs={{0,16},{1,17},{2,18},{3,19},{4,20},{5,21},{6,22},{7,23},{8,24},{9,... | collective-permute-start | bytes 331784 | tf_op jit(solution)/shard_map/ppermute | solution.py:81
  496.2 8.1 %collective-permute-start.20 = (bf16[144,384]{1,0:T(8,128)(2,1)S(1)}, bf16[144,384]{1,0:T(8,128)(2,1)S(1)}, u32[]{:S(2)}, u32[]{:S(2)}) collective-permute-start(bf16[144,384]{1,0:T(8,128)(2,1)S(1)} %dynamic-slice_add_fusion.9), channel_id=1, source_target_pairs={{0,16},{1,17},{2,18},{3,19},{4,20},{5,21},{6,22},{7,23},{8,24},{9,... | collective-permute-start | bytes 331784 | tf_op jit(solution)/shard_map/ppermute | solution.py:81
  501.9 6.2 collective-permute-start.30
  504.3 8.4 %collective-permute-start.21 = (bf16[288,384]{1,0:T(8,128)(2,1)S(1)}, bf16[288,384]{1,0:T(8,128)(2,1)S(1)}, u32[]{:S(2)}, u32[]{:S(2)}) collective-permute-start(bf16[288,384]{1,0:T(8,128)(2,1)S(1)} %pad_maximum_fusion.18), channel_id=1, source_target_pairs={{0,8},{1,9},{2,10},{3,11},{4,12},{5,13},{6,14},{7,15},{8,0},{9,1},... | collective-permute-start | bytes 663560 | tf_op jit(solution)/shard_map/ppermute | solution.py:81
  508.1 6.9 collective-permute-start.31
  512.8 12.1 %collective-permute-start.22 = (bf16[576,384]{1,0:T(8,128)(2,1)S(1)}, bf16[576,384]{1,0:T(8,128)(2,1)S(1)}, u32[]{:S(2)}, u32[]{:S(2)}) collective-permute-start(bf16[576,384]{1,0:T(8,128)(2,1)S(1)} %pad_maximum_fusion.13), channel_id=1, source_target_pairs={{0,4},{1,5},{2,6},{3,7},{4,0},{5,1},{6,2},{7,3},{8,12},{9,13},{10,... | collective-permute-start | bytes 1327112 | tf_op jit(solution)/shard_map/ppermute | solution.py:81
  515.2 14.5 %collective-permute-start.32 = (bf16[576,384]{1,0:T(8,128)(2,1)S(1)}, bf16[576,384]{1,0:T(8,128)(2,1)S(1)}, u32[]{:S(2)}, u32[]{:S(2)}) collective-permute-start(bf16[576,384]{1,0:T(8,128)(2,1)S(1)} %pad_maximum_fusion.14), channel_id=1, source_target_pairs={{0,4},{1,5},{2,6},{3,7},{4,0},{5,1},{6,2},{7,3},{8,12},{9,13},{10,... | collective-permute-start | bytes 1327112 | tf_op jit(solution)/shard_map/ppermute | solution.py:81
  525.2 21.3 %collective-permute-start.23 = (bf16[1152,384]{1,0:T(8,128)(2,1)S(1)}, bf16[1152,384]{1,0:T(8,128)(2,1)S(1)}, u32[]{:S(2)}, u32[]{:S(2)}) collective-permute-start(bf16[1152,384]{1,0:T(8,128)(2,1)S(1)} %pad_maximum_fusion.9), channel_id=1, source_target_pairs={{0,2},{1,3},{2,0},{3,1},{4,6},{5,7},{6,4},{7,5},{8,10},{9,11},{10,... | collective-permute-start | bytes 2654216 | tf_op jit(solution)/shard_map/ppermute | solution.py:81
  529.9 26.0 %collective-permute-start.33 = (bf16[1152,384]{1,0:T(8,128)(2,1)S(1)}, bf16[1152,384]{1,0:T(8,128)(2,1)S(1)}, u32[]{:S(2)}, u32[]{:S(2)}) collective-permute-start(bf16[1152,384]{1,0:T(8,128)(2,1)S(1)} %pad_maximum_fusion.10), channel_id=1, source_target_pairs={{0,2},{1,3},{2,0},{3,1},{4,6},{5,7},{6,4},{7,5},{8,10},{9,11},{10,... | collective-permute-start | bytes 2654216 | tf_op jit(solution)/shard_map/ppermute | solution.py:81
  548.2 16.5 %collective-permute-start.24 = (bf16[2304,384]{1,0:T(8,128)(2,1)}, bf16[2304,384]{1,0:T(8,128)(2,1)}, u32[]{:S(2)}, u32[]{:S(2)}) collective-permute-start(bf16[2304,384]{1,0:T(8,128)(2,1)} %pad_maximum_fusion.5), channel_id=1, source_target_pairs={{0,1},{1,0},{2,3},{3,2},{4,5},{5,4},{6,7},{7,6},{8,9},{9,8},{10,11... | collective-permute-start | bytes 5308424 | tf_op jit(solution)/shard_map/ppermute | solution.py:81
  557.8 11.1 %collective-permute-start.34 = (bf16[2304,384]{1,0:T(8,128)(2,1)}, bf16[2304,384]{1,0:T(8,128)(2,1)}, u32[]{:S(2)}, u32[]{:S(2)}) collective-permute-start(bf16[2304,384]{1,0:T(8,128)(2,1)} %pad_maximum_fusion.6), channel_id=1, source_target_pairs={{0,1},{1,0},{2,3},{3,2},{4,5},{5,4},{6,7},{7,6},{8,9},{9,8},{10,11... | collective-permute-start | bytes 5308424 | tf_op jit(solution)/shard_map/ppermute | solution.py:81
  563.4 67.5 %collective-permute-start.36 = (bf16[2,2,2,64,2944]{4,3,2,1,0:T(8,128)(2,1)S(1)}, bf16[2,2,2,64,2944]{4,3,2,1,0:T(8,128)(2,1)S(1)}, u32[]{:S(2)}, u32[]{:S(2)}) collective-permute-start(bf16[2,2,2,64,2944]{4,3,2,1,0:T(8,128)(2,1)S(1)} %dynamic-slice_bitcast_fusion.1), channel_id=1, source_target_pairs={{0,2},{1,3},{2,0},{3,1},{4,6},{5,7},{6,4},{7,5},{8,10},{9,11},{10,... | collective-permute-start | bytes 9043976 | tf_op jit(solution)/shard_map/ppermute | solution.py:81
  575.7 55.5 %copy-start.4 = (f32[4608,384]{1,0:T(8,128)}, f32[4608,384]{1,0:T(8,128)S(1)}, u32[]{:S(2)}) copy-start(f32[4608,384]{1,0:T(8,128)S(1)} %maximum_convert_fusion.1) | copy-start | bytes 21233668
  632.9 34.4 %collective-permute-start.37 = (bf16[2,2,64,2944]{3,2,1,0:T(8,128)(2,1)S(1)}, bf16[2,2,64,2944]{3,2,1,0:T(8,128)(2,1)S(1)}, u32[]{:S(2)}, u32[]{:S(2)}) collective-permute-start(bf16[2,2,64,2944]{3,2,1,0:T(8,128)(2,1)S(1)} %dynamic-slice_bitcast_fusion.2), channel_id=1, source_target_pairs={{0,4},{1,5},{2,6},{3,7},{4,0},{5,1},{6,2},{7,3},{8,12},{9,13},{10,... | collective-permute-start | bytes 4521992 | tf_op jit(solution)/shard_map/ppermute | solution.py:81
  645.8 21.5 %copy-start.16 = (bf16[2,2,2,64,2944]{4,3,2,1,0:T(8,128)(2,1)S(1)}, bf16[2,2,2,64,2944]{4,3,2,1,0:T(8,128)(2,1)}, u32[]{:S(2)}) copy-start(bf16[2,2,2,64,2944]{4,3,2,1,0:T(8,128)(2,1)} %copy-done.15) | copy-start | bytes 9043972
  668.4 17.6 %collective-permute-start.38 = (bf16[2,64,2944]{2,1,0:T(8,128)(2,1)}, bf16[2,64,2944]{2,1,0:T(8,128)(2,1)}, u32[]{:S(2)}, u32[]{:S(2)}) collective-permute-start(bf16[2,64,2944]{2,1,0:T(8,128)(2,1)} %dynamic-slice_bitcast_fusion.3), channel_id=1, source_target_pairs={{0,8},{1,9},{2,10},{3,11},{4,12},{5,13},{6,14},{7,15},{8,0},{9,1},... | collective-permute-start | bytes 2261000 | tf_op jit(solution)/shard_map/ppermute | solution.py:81
  687.2 17.3 %collective-permute-start.39 = (bf16[64,2944]{1,0:T(8,128)(2,1)S(1)}, bf16[64,2944]{1,0:T(8,128)(2,1)S(1)}, u32[]{:S(2)}, u32[]{:S(2)}) collective-permute-start(bf16[64,2944]{1,0:T(8,128)(2,1)S(1)} %dynamic-slice_bitcast_fusion.4), channel_id=1, source_target_pairs={{0,16},{1,17},{2,18},{3,19},{4,20},{5,21},{6,22},{7,23},{8,24},{9,... | collective-permute-start | bytes 1130504 | tf_op jit(solution)/shard_map/ppermute | solution.py:81
  687.9 19.5 %copy-start.1 = (bf16[384,2048]{1,0:T(8,128)(2,1)S(1)}, bf16[384,2048]{1,0:T(8,128)(2,1)}, u32[]{:S(2)}) copy-start(bf16[384,2048]{1,0:T(8,128)(2,1)} %param.36) | copy-start | bytes 4718596
  (72 other events, 275.2 us)
